TPU v7x, 32 devices: a whole 2x2x4 slice. The times are simulated.
32 devices in a mesh: walk: 8 (over z, x), chol: 4 (over y, core).
Axes of the slice: x: 2, y: 2, z: 4, core: 2. Of those that a mesh axis runs over, the one named last changes fastest.
Arguments:
- walkers: bfloat16 [48, 2048, 128], P('walk', 'chol'), may hold values from -6 to 6
- inv_intersection: bfloat16 [48, 128, 128], P('walk'), may hold values from -0.5 to 0.5
- fields: bfloat16 [48, 8], P('walk', 'chol'), may hold values from -5 to 5
- cholesky: bfloat16 [8, 256, 2048], P('chol'), may hold values from -0.125 to 0.125
- trial_rows: bfloat16 [256, 128], replicated, may hold values from -0.33007812 to 0.33007812
- counts: int32 [8], replicated, may hold values from 1 to 6, as said below
- partner: int32 [8], replicated, may hold values from 0 to 7, as said below
Outputs:
- new_walkers: bfloat16 [32, 256, 128], P('walk', 'chol')
- log_weight: float32 [32], P('walk')
Inputs may be any that keep to these rules, and one draw needn't show every extreme that they name: `counts`: of w and partner[w], exactly one holds more than 4 walkers, and the other holds at most 8 minus that count; some walk index holds exactly 6 walkers. partner[partner[w]] = w, and partner[w] differs from w in exactly one bit.
All inputs are finite; a program needn't handle non-finite values.
Results may differ from a plain program's by a relative error of at most 0.0075.
Values may be sent and summed in bfloat16 or wider, within the bound.
A program may use at most 64 MiB of HBM per device.

v0:
```python
import jax
import jax.numpy as jnp
from jax import lax
from jax.sharding import PartitionSpec as P

ROWS_DEV = 64
LIVE = 4
MOVE = 2


STEP_ROOT = 0.1


def from_partner(block, axis, distance):
    count = lax.axis_size(axis)
    route = []
    for low in range(count):
        high = low | 1 << distance
        if high != low and high < count:
            route += [(low, high), (high, low)]
    return lax.ppermute(block, axis, route)


def expand_mask(mask_in, target):
    return mask_in.reshape(mask_in.shape + (1,) * (target.ndim - mask_in.ndim))


def select_slots(own_part, arriving, own_mask, incoming):
    arrived = jnp.zeros_like(own_part)
    for slot_num in range(MOVE):
        flag = incoming[:, slot_num]
        arrived = jnp.where(expand_mask(flag, own_part), arriving[slot_num : slot_num + 1], arrived)
    return jnp.where(expand_mask(own_mask, own_part), own_part, arrived)


def propagate(walker_rows, minv, field_part, cholesky, trial_rows):
    products = jnp.einsum(
        "grk,wkn->wgrn",
        cholesky,
        lax.all_gather(walker_rows, "chol", axis=1, tiled=True),
        preferred_element_type=jnp.float32,
    )
    weighted = jnp.einsum("rb,wab->wra", trial_rows, minv, preferred_element_type=jnp.float32)
    force_bias = -STEP_ROOT * jnp.einsum("wgrn,wrn->wg", products, weighted)
    field_wide = field_part.astype(jnp.float32)
    shifted = STEP_ROOT * (field_wide - force_bias)
    row_terms = jnp.einsum("wg,wgrn->wrn", shifted, products)
    weight_terms = jnp.sum(field_wide * force_bias - 0.5 * force_bias * force_bias, axis=1)
    increment = lax.psum_scatter(row_terms, "chol", scatter_dimension=1, tiled=True)
    log_terms = lax.psum(weight_terms, "chol")
    window = walker_rows[:, :ROWS_DEV, :].astype(jnp.float32)
    return (window + increment, log_terms)


def shards(walkers, inv_intersection, fields, cholesky, trial_rows, counts, partner):
    walk_index = lax.axis_index("walk")
    own_count = counts[walk_index]
    mate_id = partner[walk_index]
    arriving_count = jnp.maximum(counts[mate_id] - LIVE, 0)
    bit_count = lax.axis_size("walk").bit_length() - 1
    slot_ids = jnp.arange(LIVE, dtype=jnp.int32)
    move_ids = jnp.arange(MOVE, dtype=jnp.int32)
    own_mask = slot_ids < jnp.minimum(own_count, LIVE)
    incoming = (slot_ids[:, None] - own_count == move_ids[None, :]) & (
        move_ids[None, :] < arriving_count
    )
    live_wide = (own_mask | jnp.any(incoming, axis=1)).astype(jnp.float32)
    all_rows, all_terms = propagate(walkers, inv_intersection, fields, cholesky, trial_rows)
    outgoing = (all_rows[LIVE:], all_terms[LIVE:])
    received = tuple((jnp.zeros_like(member) for member in outgoing))
    for bit_num in range(bit_count):
        fetched = (
            from_partner(outgoing[0].astype(jnp.bfloat16), "walk", bit_num).astype(jnp.float32),
            from_partner(outgoing[1].astype(jnp.bfloat16), "walk", bit_num).astype(jnp.float32),
        )
        active = jnp.bitwise_xor(mate_id, walk_index) == 1 << bit_num
        received = tuple(
            (jnp.where(active, new_part, old_part) for new_part, old_part in zip(fetched, received))
        )
    new_rows = select_slots(all_rows[:LIVE], received[0], own_mask, incoming)
    log_terms = select_slots(all_terms[:LIVE], received[1], own_mask, incoming)
    new_walkers = (live_wide[:, None, None] * new_rows).astype(jnp.bfloat16)
    return (new_walkers, live_wide * log_terms)


def solution(mesh):
    in_specs = (
        P("walk", "chol", None),
        P("walk", None, None),
        P("walk", "chol"),
        P("chol", None, None),
        P(),
        P(),
        P(),
    )
    out_specs = (P("walk", "chol", None), P("walk"))
    return jax.shard_map(shards, mesh=mesh, in_specs=in_specs, out_specs=out_specs, check_vma=False)
```

profile of v0, /device:TPU:0, one launch (start us, length us, event | category | flops | bytes accessed | tf_op | source)
XLA Modules:
  0.0 91.6 jit_solution(14081499370245136557)
XLA Ops:
  7.2 0.0 copy-start
  7.2 0.0 copy-start.2
  7.2 0.0 copy-start.3
  7.2 0.0 all-gather.2.cloned.1.call-start
  7.2 2.5 %copy.9 = bf16[6,512,128]{1,2,0:T(8,128)(2,1)} copy(bf16[6,512,128]{2,1,0:T(8,128)(2,1)} %param.7) | data formatting | bytes 1572864 | tf_op args[0]
  9.7 0.0 all-gather.2.cloned.1.call-update
  9.7 0.0 reduce-scatter.2.cloned.1.call-start
  9.8 0.0 copy-done.2
  9.8 0.0 copy-done.3
  9.8 0.3 convolution_bitcast_fusion
  10.1 31.1 %all-gather.2.cloned.1.call-done = bf16[6,2048,128]{1,2,0:T(8,128)(2,1)} async-done(((bf16[6,512,128]{1,2,0:T(8,128)(2,1)}), bf16[6,2048,128]{1,2,0:T(8,128)(2,1)}) %all-gather.2.cloned.1.call-update) | async-done | bytes 3145744 | tf_op jit(solution)/shard_map/all_gather | solution.py:40
  41.1 0.0 copy-done
  41.1 3.7 %fusion.5 = f32[6,2,256,128]{2,3,1,0:T(8,128)S(1)} fusion(bf16[2,256,2048]{2,1,0:T(8,128)(2,1)S(1)} %copy-done, bf16[6,2048,128]{1,2,0:T(8,128)(2,1)} %all-gather.2.cloned.1.call-done), kind=kOutput, calls=%fused_computation.6 | convolution fusion | flops 1610612736 | bytes 6815744 | tf_op jit(solution)/shard_map/grk,wkn->wgrn/dot_general | solution.py:37
  44.8 0.0 copy-start.1
  44.8 1.1 %copy-done.1 = f32[6,2,256,128]{2,3,1,0:T(8,128)} copy-done((f32[6,2,256,128]{2,3,1,0:T(8,128)}, f32[6,2,256,128]{2,3,1,0:T(8,128)S(1)}, u32[]{:S(2)}) %copy-start.1) | copy-done | bytes 1572888
  46.0 0.0 copy-start.5
  46.0 2.3 %fusion.3 = f32[6,1,2,1]{2,1,3,0:T(1,128)S(1)} fusion(f32[6,2,256,128]{2,3,1,0:T(8,128)S(1)} %fusion.5, bf16[6,256,128,1]{1,2,0,3:T(8,128)(2,1)S(1)} %convolution_bitcast_fusion), kind=kOutput, calls=%fused_computation.4 | convolution fusion | flops 786432 | bytes 1966128 | tf_op jit(solution)/shard_map/wgrn,wrn->wg/dot_general | solution.py:44
  48.2 0.1 copy.13
  48.3 0.0 copy-done.5
  48.4 0.1 copy.19
  48.5 1.7 %multiply_reduce_fusion = f32[6,256,128]{1,2,0:T(8,128)S(1)} fusion(f32[6,2,256,128]{2,3,1,0:T(8,128)} %copy-done.1, f32[6,2]{1,0:T(8,128)S(1)} %copy.19), kind=kLoop, calls=%fused_computation.3 | loop fusion | flops 589824 | bytes 2359344
  50.2 1.2 %copy.18 = f32[6,256,128]{2,1,0:T(8,128)} copy(f32[6,256,128]{1,2,0:T(8,128)S(1)} %multiply_reduce_fusion) | data formatting | bytes 1572864 | tf_op jit(solution)/shard_map/wg,wgrn->wrn/dot_general | solution.py:47
  51.4 0.0 reduce-scatter.2.cloned.1.call-update
  51.4 0.0 copy-done.6
  51.4 0.6 dynamic_slice.10
  54.6 0.0 copy-done.4
  54.6 0.6 fusion.20
  56.5 0.7 iota_subtract_fusion
  57.2 0.1 fusion.18
  57.3 5.9 %psum.7 = f32[6]{0:T(128)S(1)} all-reduce(f32[6]{0:T(128)S(1)} %get-tuple-element.6), channel_id=1, replica_groups=mesh['walk'=8,'chol'=4] {'chol'}, use_global_device_ids=true, to_apply=%region_3.0 | all-reduce | flops 6 | bytes 48 | tf_op jit(solution)/shard_map/psum | solution.py:50
  63.2 0.1 slice.45
  63.2 1.6 %collective-permute-start.5 = (bf16[2]{0:T(256)(128)(2,1)S(1)}, bf16[2]{0:T(256)(128)(2,1)S(1)}, u32[]{:S(2)}, u32[]{:S(2)}) collective-permute-start(bf16[2]{0:T(256)(128)(2,1)S(1)} %slice.45), channel_id=1, source_target_pairs={{0,4},{4,0},{8,12},{12,8},{16,20},{20,16},{24,28},{28,24},{1,5},{5... | collective-permute-start | bytes 20 | tf_op jit(solution)/shard_map/ppermute | solution.py:21
  64.9 1.5 %collective-permute-start.4 = (bf16[2]{0:T(256)(128)(2,1)S(1)}, bf16[2]{0:T(256)(128)(2,1)S(1)}, u32[]{:S(2)}, u32[]{:S(2)}) collective-permute-start(bf16[2]{0:T(256)(128)(2,1)S(1)} %slice.45), channel_id=1, source_target_pairs={{0,8},{8,0},{4,12},{12,4},{16,24},{24,16},{20,28},{28,20},{1,9},{9... | collective-permute-start | bytes 20 | tf_op jit(solution)/shard_map/ppermute | solution.py:21
  66.4 2.4 %collective-permute-start.3 = (bf16[2]{0:T(256)(128)(2,1)S(1)}, bf16[2]{0:T(256)(128)(2,1)S(1)}, u32[]{:S(2)}, u32[]{:S(2)}) collective-permute-start(bf16[2]{0:T(256)(128)(2,1)S(1)} %slice.45), channel_id=1, source_target_pairs={{0,16},{16,0},{4,20},{20,4},{8,24},{24,8},{12,28},{28,12},{1,17},{... | collective-permute-start | bytes 20 | tf_op jit(solution)/shard_map/ppermute | solution.py:21
  68.8 0.0 collective-permute-done.5
  68.8 0.0 collective-permute-done.4
  68.8 2.0 %collective-permute-done.3 = bf16[2]{0:T(256)(128)(2,1)S(1)} collective-permute-done((bf16[2]{0:T(256)(128)(2,1)S(1)}, bf16[2]{0:T(256)(128)(2,1)S(1)}, u32[]{:S(2)}, u32[]{:S(2)}) %collective-permute-start.3) | collective-permute-done | bytes 36 | tf_op jit(solution)/shard_map/ppermute | solution.py:21
  70.8 0.6 fusion.19
  71.4 3.4 %reduce-scatter.2.cloned.1.call-done = f32[6,64,128]{2,1,0:T(8,128)} async-done(((f32[6,256,128]{2,1,0:T(8,128)}), f32[6,64,128]{2,1,0:T(8,128)}) %reduce-scatter.2.cloned.1.call-update) | async-done | bytes 196624 | tf_op jit(solution)/shard_map/reduce_scatter | solution.py:49
  74.8 1.0 %convert_add_fusion = f32[6,64,128]{2,1,0:T(8,128)S(1)} fusion(f32[6,64,128]{2,1,0:T(8,128)} %reduce-scatter.2.cloned.1.call-done, bf16[6,512,128]{2,1,0:T(8,128)(2,1)} %param.7), kind=kLoop, calls=%fused_computation.9 | loop fusion | flops 98304 | bytes 491520 | tf_op jit(solution)/shard_map/add | solution.py:52
  75.8 1.5 %collective-permute-start.2 = (bf16[2,64,128]{2,1,0:T(8,128)(2,1)S(1)}, bf16[2,64,128]{2,1,0:T(8,128)(2,1)S(1)}, u32[]{:S(2)}, u32[]{:S(2)}) collective-permute-start(bf16[2,64,128]{2,1,0:T(8,128)(2,1)S(1)} %slice.68), channel_id=1, source_target_pairs={{0,4},{4,0},{8,12},{12,8},{16,20},{20,16},{24,28},{28,24},{1,5},{5... | collective-permute-start | bytes 98312 | tf_op jit(solution)/shard_map/ppermute | solution.py:21
  77.4 1.5 %collective-permute-start.1 = (bf16[2,64,128]{2,1,0:T(8,128)(2,1)S(1)}, bf16[2,64,128]{2,1,0:T(8,128)(2,1)S(1)}, u32[]{:S(2)}, u32[]{:S(2)}) collective-permute-start(bf16[2,64,128]{2,1,0:T(8,128)(2,1)S(1)} %slice.68), channel_id=1, source_target_pairs={{0,8},{8,0},{4,12},{12,4},{16,24},{24,16},{20,28},{28,20},{1,9},{9... | collective-permute-start | bytes 98312 | tf_op jit(solution)/shard_map/ppermute | solution.py:21
  78.9 2.4 %collective-permute-start = (bf16[2,64,128]{2,1,0:T(8,128)(2,1)S(1)}, bf16[2,64,128]{2,1,0:T(8,128)(2,1)S(1)}, u32[]{:S(2)}, u32[]{:S(2)}) collective-permute-start(bf16[2,64,128]{2,1,0:T(8,128)(2,1)S(1)} %slice.68), channel_id=1, source_target_pairs={{0,16},{16,0},{4,20},{20,4},{8,24},{24,8},{12,28},{28,12},{1,17},{... | collective-permute-start | bytes 98312 | tf_op jit(solution)/shard_map/ppermute | solution.py:21
  81.2 1.8 %select_select_fusion.1 = f32[4]{0:T(128)} fusion(f32[6]{0:T(128)S(1)} %psum.7, f32[]{:T(128)} %bitcast.16, f32[]{:T(128)} %bitcast.15, pred[4]{0:T(512)(128)(4,1)S(1)} %get-tuple-element.2, pred[4,2]{0,1:T(4,128)(4,1)S(1)} %get-tuple-element.3, s32[]{:T(128)S(6)} %min.3), kind=kLoop, calls=%fused_computation.32 | loop fusion | flops 24 | bytes 56 | tf_op jit(solution)/shard_map/mul | solution.py:83
  83.0 0.0 collective-permute-done.2
  83.0 0.0 collective-permute-done.1
  83.0 0.9 %collective-permute-done = bf16[2,64,128]{2,1,0:T(8,128)(2,1)S(1)} collective-permute-done((bf16[2,64,128]{2,1,0:T(8,128)(2,1)S(1)}, bf16[2,64,128]{2,1,0:T(8,128)(2,1)S(1)}, u32[]{:S(2)}, u32[]{:S(2)}) %collective-permute-start) | collective-permute-done | bytes 32800 | tf_op jit(solution)/shard_map/ppermute | solution.py:21
  84.0 0.7 fusion.12
  (11 shorter events, 0.1 us)
Async XLA Ops:
  7.2 33.9 %copy-start = (bf16[2,256,2048]{2,1,0:T(8,128)(2,1)S(1)}, bf16[2,256,2048]{2,1,0:T(8,128)(2,1)}, u32[]{:S(2)}) copy-start(bf16[2,256,2048]{2,1,0:T(8,128)(2,1)} %param.10) | copy-start | bytes 6291460
  7.2 2.6 %copy-start.2 = (bf16[6,128,128]{2,1,0:T(8,128)(2,1)S(1)}, bf16[6,128,128]{2,1,0:T(8,128)(2,1)}, u32[]{:S(2)}) copy-start(bf16[6,128,128]{2,1,0:T(8,128)(2,1)} %param.8) | copy-start | bytes 589828
  7.2 2.6 %copy-start.3 = (bf16[256,128]{1,0:T(8,128)(2,1)S(1)}, bf16[256,128]{1,0:T(8,128)(2,1)}, u32[]{:S(2)}) copy-start(bf16[256,128]{1,0:T(8,128)(2,1)} %param.11) | copy-start | bytes 196612
  7.2 33.9 %all-gather.2.cloned.1.call-start = ((), (), s32[]{:S(2)}) async-start(), calls=%async_computation.1 | async-start | bytes 3932160 | tf_op jit(solution)/shard_map/all_gather | solution.py:40
  9.7 65.1 %reduce-scatter.2.cloned.1.call-start = ((), (), s32[]{:S(2)}) async-start(), calls=%async_computation.2 | async-start | bytes 983040 | tf_op jit(solution)/shard_map/reduce_scatter | solution.py:49
  44.8 1.2 %copy-start.1 = (f32[6,2,256,128]{2,3,1,0:T(8,128)}, f32[6,2,256,128]{2,3,1,0:T(8,128)S(1)}, u32[]{:S(2)}) copy-start(f32[6,2,256,128]{2,3,1,0:T(8,128)S(1)} %fusion.5) | copy-start | bytes 4718596
  46.0 2.4 %copy-start.5 = (bf16[6,2]{0,1:T(2,128)(2,1)S(1)}, bf16[6,2]{0,1:T(2,128)(2,1)}, u32[]{:S(2)}) copy-start(bf16[6,2]{0,1:T(2,128)(2,1)} %param.9) | copy-start | bytes 76
  48.5 2.9 %copy-start.6 = (s32[8]{0:T(128)S(1)}, s32[8]{0:T(128)}, u32[]{:S(2)}) copy-start(s32[8]{0:T(128)} %param.13) | copy-start | bytes 100
  48.5 6.1 %copy-start.4 = (s32[8]{0:T(128)S(1)}, s32[8]{0:T(128)}, u32[]{:S(2)}) copy-start(s32[8]{0:T(128)} %param.12) | copy-start | bytes 100
  63.2 5.5 %collective-permute-start.5 = (bf16[2]{0:T(256)(128)(2,1)S(1)}, bf16[2]{0:T(256)(128)(2,1)S(1)}, u32[]{:S(2)}, u32[]{:S(2)}) collective-permute-start(bf16[2]{0:T(256)(128)(2,1)S(1)} %slice.45), channel_id=1, source_target_pairs={{0,4},{4,0},{8,12},{12,8},{16,20},{20,16},{24,28},{28,24},{1,5},{5... | collective-permute-start | bytes 20 | tf_op jit(solution)/shard_map/ppermute | solution.py:21
  64.9 3.9 %collective-permute-start.4 = (bf16[2]{0:T(256)(128)(2,1)S(1)}, bf16[2]{0:T(256)(128)(2,1)S(1)}, u32[]{:S(2)}, u32[]{:S(2)}) collective-permute-start(bf16[2]{0:T(256)(128)(2,1)S(1)} %slice.45), channel_id=1, source_target_pairs={{0,8},{8,0},{4,12},{12,4},{16,24},{24,16},{20,28},{28,20},{1,9},{9... | collective-permute-start | bytes 20 | tf_op jit(solution)/shard_map/ppermute | solution.py:21
  66.4 4.4 %collective-permute-start.3 = (bf16[2]{0:T(256)(128)(2,1)S(1)}, bf16[2]{0:T(256)(128)(2,1)S(1)}, u32[]{:S(2)}, u32[]{:S(2)}) collective-permute-start(bf16[2]{0:T(256)(128)(2,1)S(1)} %slice.45), channel_id=1, source_target_pairs={{0,16},{16,0},{4,20},{20,4},{8,24},{24,8},{12,28},{28,12},{1,17},{... | collective-permute-start | bytes 20 | tf_op jit(solution)/shard_map/ppermute | solution.py:21
  75.8 7.2 %collective-permute-start.2 = (bf16[2,64,128]{2,1,0:T(8,128)(2,1)S(1)}, bf16[2,64,128]{2,1,0:T(8,128)(2,1)S(1)}, u32[]{:S(2)}, u32[]{:S(2)}) collective-permute-start(bf16[2,64,128]{2,1,0:T(8,128)(2,1)S(1)} %slice.68), channel_id=1, source_target_pairs={{0,4},{4,0},{8,12},{12,8},{16,20},{20,16},{24,28},{28,24},{1,5},{5... | collective-permute-start | bytes 98312 | tf_op jit(solution)/shard_map/ppermute | solution.py:21
  77.4 5.7 %collective-permute-start.1 = (bf16[2,64,128]{2,1,0:T(8,128)(2,1)S(1)}, bf16[2,64,128]{2,1,0:T(8,128)(2,1)S(1)}, u32[]{:S(2)}, u32[]{:S(2)}) collective-permute-start(bf16[2,64,128]{2,1,0:T(8,128)(2,1)S(1)} %slice.68), channel_id=1, source_target_pairs={{0,8},{8,0},{4,12},{12,4},{16,24},{24,16},{20,28},{28,20},{1,9},{9... | collective-permute-start | bytes 98312 | tf_op jit(solution)/shard_map/ppermute | solution.py:21
  78.9 5.1 %collective-permute-start = (bf16[2,64,128]{2,1,0:T(8,128)(2,1)S(1)}, bf16[2,64,128]{2,1,0:T(8,128)(2,1)S(1)}, u32[]{:S(2)}, u32[]{:S(2)}) collective-permute-start(bf16[2,64,128]{2,1,0:T(8,128)(2,1)S(1)} %slice.68), channel_id=1, source_target_pairs={{0,16},{16,0},{4,20},{20,4},{8,24},{24,8},{12,28},{28,12},{1,17},{... | collective-permute-start | bytes 98312 | tf_op jit(solution)/shard_map/ppermute | solution.py:21
Sparse Core Ops, SparseCore 0:
  9.8 31.2 all-gather.1
  51.5 23.2 reduce-scatter.1
where the time goes:
time: 91.9 us; the launch traced here: 91.6 us
  waiting for transfers between devices  37.5 us (41%)
  between operations  18.1 us (20%)
  starting transfers between devices  11 us (12%)
  local copies, waits for them, and re-layouts  6.84 us (7%)
  matrix products  6.23 us (7%)
  other arithmetic  6.05 us (7%)
  blocking collectives  5.9 us (6%)
    all_gather x1, waiting for transfers between devices, propagate(): lax.all_gather(walker_rows, 'chol', axis=1, tiled=True)  31.1 us
    ppermute x6, starting transfers between devices, from_partner(): return lax.ppermute(block, axis, route)  10.9 us
    psum x1, blocking collectives, propagate(): log_terms = lax.psum(weight_terms, 'chol')  5.9 us
    unnamed x16, local copies, waits for them, and re-layouts  3.72 us
    dot_general x1, matrix products, propagate(): jnp.einsum('grk,wkn->wgrn', cholesky, lax.all_gather(walker_rows, 'chol',...  3.7 us
    reduce_scatter x1, waiting for transfers between devices, propagate(): lax.psum_scatter(row_terms, 'chol', scatter_dimension=1, tiled=True)  3.4 us
    ppermute x6, waiting for transfers between devices, from_partner(): return lax.ppermute(block, axis, route)  2.98 us
    dot_general x1, matrix products, propagate(): force_bias = -STEP_ROOT * jnp.einsum('wgrn,wrn->wg', products, weighted)  2.27 us
  transfers between devices with their start and end apart: 8, of which 4 were waited for; matrix products, arithmetic and copies ran while one was open for 5% of the time, Pallas kernels for 0%

commit v1 on v0

v1 whole, which is shorter than its diff:
```python
import functools

import jax
import jax.numpy as jnp
from jax import lax
from jax.experimental import pallas as pl
from jax.experimental.pallas import tpu as pltpu
from jax.sharding import PartitionSpec as P

LIVE = 4
MOVE = 2
STEP_ROOT = 0.1
LOG_ROWS = 8
TAIL = 2 * LOG_ROWS
MESH = pl.DeviceIdType.MESH


def pick(flag, chosen, other):
    mask = jnp.broadcast_to(flag.astype(jnp.int32), chosen.shape) > 0
    return jnp.where(mask, chosen, other)


def kernel(
    chol_count,
    bit_count,
    walkers,
    minv_in,
    fields,
    chol_in,
    trial_in,
    counts,
    partner,
    new_out,
    log_out,
    phi,
    chol,
    minv,
    trial,
    prod,
    weighted,
    terms,
    logs,
    mine,
    sib_out,
    sib_in,
    far_out,
    far_in,
    moved_out,
    moved_in,
    load_sem,
    near_sem,
    ahead_send,
    ahead_recv,
    pass_send,
    pass_recv,
    sib_send,
    sib_recv,
    far_send,
    far_recv,
    moved_send,
    moved_recv,
):
    slots, depth, occ = walkers.shape
    vectors, rows, _ = chol_in.shape
    own_rows = rows // chol_count
    half = chol_count // 2
    walk = lax.axis_index("walk")
    me = lax.axis_index("chol")
    high, low = me // 2, me % 2
    sibling = 2 * high + 1 - low
    far_ids = [2 * lax.rem(high + step, half) + low for step in range(1, half)]
    from_high = [lax.rem(high - step + half, half) for step in range(1, half)]
    mates = [jnp.bitwise_xor(walk, 1 << bit) for bit in range(bit_count)]

    loads = [
        pltpu.make_async_copy(walkers, phi.at[:, me], load_sem.at[0]),
        pltpu.make_async_copy(chol_in, chol, load_sem.at[1]),
        pltpu.make_async_copy(minv_in, minv, load_sem.at[2]),
        pltpu.make_async_copy(trial_in, trial, load_sem.at[3]),
    ]
    for load in loads:
        load.start()

    barrier = pltpu.get_barrier_semaphore()
    peers = [{"chol": sibling}] + [{"chol": far} for far in far_ids] + [{"walk": mate} for mate in mates]
    for peer in peers:
        pl.semaphore_signal(barrier, inc=1, device_id=peer, device_id_type=MESH)
    pl.semaphore_wait(barrier, len(peers))

    def remote(src, dst, send, recv, peer):
        return pltpu.make_async_remote_copy(
            src_ref=src, dst_ref=dst, send_sem=send, recv_sem=recv, device_id=peer, device_id_type=MESH
        )

    order = list(range(LIVE, slots)) + list(range(LIVE))
    ahead = {}
    for slot in order:
        for step in range(half - 1):
            ahead[slot, step] = remote(
                walkers.at[slot],
                phi.at[slot, me],
                ahead_send.at[slot, step],
                ahead_recv.at[slot, step],
                {"chol": far_ids[step]},
            )
            ahead[slot, step].start()
    near = remote(walkers, phi.at[:, me], near_sem.at[0], near_sem.at[1], {"chol": sibling})
    near.start()

    for load in loads[2:]:
        load.wait()
    for slot in range(slots):
        weighted[slot] = lax.dot_general(
            trial[...], minv[slot], (((1,), (1,)), ((), ())), preferred_element_type=jnp.float32
        )
    for load in loads[:2]:
        load.wait()
    near.wait_recv()

    def chol_half(index):
        columns = pl.ds(pl.multiple_of(index * 2 * depth, 2 * depth), 2 * depth)
        return chol[:, :, columns].reshape(vectors * rows, 2 * depth)

    def phi_half(slot, index):
        return phi[slot, pl.ds(2 * index, 2)].reshape(2 * depth, occ)

    @pl.loop(0, slots // 2)
    def _(pair):
        both = jnp.concatenate([phi_half(2 * pair, high), phi_half(2 * pair + 1, high)], axis=1)
        result = jnp.dot(chol_half(high), both, preferred_element_type=jnp.float32)
        prod[2 * pair] = result[:, :occ]
        prod[2 * pair + 1] = result[:, occ:]

    field_wide = fields[...].astype(jnp.float32)

    def multiply(slot):
        passed = []
        for step in range(half - 1):
            ahead[slot, step].wait_recv()
            block = phi.at[slot, 2 * from_high[step] + low]
            passed.append(
                remote(block, block, pass_send.at[slot, step], pass_recv.at[slot, step], {"chol": sibling})
            )
            passed[step].start()
        total = prod[slot]
        for step in range(half - 1):
            passed[step].wait_recv()
            total += jnp.dot(
                chol_half(from_high[step]),
                phi_half(slot, from_high[step]),
                preferred_element_type=jnp.float32,
            )
        total = total.reshape(vectors, rows, occ)
        increment = jnp.zeros((rows, occ), jnp.float32)
        weight = jnp.zeros((1, 1), jnp.float32)
        for vector in range(vectors):
            force_bias = -STEP_ROOT * jnp.sum(total[vector] * weighted[slot], keepdims=True)
            field = field_wide[slot : slot + 1, vector : vector + 1]
            increment += (STEP_ROOT * (field - force_bias)) * total[vector]
            weight += field * force_bias - 0.5 * force_bias * force_bias
        terms[slot] = increment.reshape(chol_count, own_rows, occ)
        logs[slot] = jnp.broadcast_to(weight, (LOG_ROWS, occ))
        for index in range(half):
            sib_out[slot, pl.ds(index * own_rows, own_rows)] = terms[slot, 2 * index + 1 - low]
        sib_out[slot, pl.ds(half * own_rows, LOG_ROWS)] = logs[slot]
        copy = remote(
            sib_out.at[slot], sib_in.at[slot], sib_send.at[slot], sib_recv.at[slot], {"chol": sibling}
        )
        copy.start()
        return passed, copy

    def chip_sum(slot, index):
        start = pl.multiple_of(index * own_rows, own_rows)
        return terms[slot, 2 * index + low] + sib_in[slot, pl.ds(start, own_rows)]

    def add_chip(slot, copy):
        copy.wait_recv()
        weight = logs[slot] + sib_in[slot, pl.ds(half * own_rows, LOG_ROWS)]
        logs[slot] = weight
        coarse = weight.astype(jnp.bfloat16).astype(jnp.float32)
        tail = jnp.concatenate([coarse, weight - coarse], axis=0).astype(jnp.bfloat16)
        copies = []
        for step in range(half - 1):
            far_out[slot, step, pl.ds(0, own_rows)] = chip_sum(slot, lax.rem(high + step + 1, half)).astype(
                jnp.bfloat16
            )
            far_out[slot, step, pl.ds(own_rows, TAIL)] = tail
            copies.append(
                remote(
                    far_out.at[slot, step],
                    far_in.at[slot, step],
                    far_send.at[slot, step],
                    far_recv.at[slot, step],
                    {"chol": far_ids[step]},
                )
            )
            copies[step].start()
        mine[slot] = chip_sum(slot, high) + phi[slot, me, pl.ds(0, own_rows)].astype(jnp.float32)
        return copies

    def split_log(tail):
        return tail[:LOG_ROWS] + tail[LOG_ROWS:]

    def finish(slot, copies):
        result, weight = mine[slot], logs[slot]
        for step in range(half - 1):
            copies[step].wait_recv()
            result += far_in[slot, step, pl.ds(0, own_rows)].astype(jnp.float32)
            weight += split_log(far_in[slot, step, pl.ds(own_rows, TAIL)].astype(jnp.float32))
        if slot < LIVE:
            mine[slot] = result
            logs[slot] = weight
        else:
            start = (slot - LIVE) * (own_rows + TAIL)
            coarse = weight.astype(jnp.bfloat16).astype(jnp.float32)
            moved_out[pl.ds(start, own_rows)] = result.astype(jnp.bfloat16)
            moved_out[pl.ds(start + own_rows, TAIL)] = jnp.concatenate(
                [coarse, weight - coarse], axis=0
            ).astype(jnp.bfloat16)

    moved = [
        remote(moved_out, moved_in.at[bit], moved_send.at[bit], moved_recv.at[bit], {"walk": mates[bit]})
        for bit in range(bit_count)
    ]
    sent, near_copies, far_copies = [near] + list(ahead.values()), {}, {}

    def later(position):
        if position - 1 >= 0 and position - 1 < slots:
            slot = order[position - 1]
            far_copies[slot] = add_chip(slot, near_copies[slot])
        if position - 2 >= 0:
            slot = order[position - 2]
            finish(slot, far_copies[slot])
            if slot == slots - 1:
                for copy in moved:
                    copy.start()

    for position in range(slots):
        slot = order[position]
        passed, near_copies[slot] = multiply(slot)
        sent += passed
        later(position)
    later(slots)
    later(slots + 1)

    for copy in sent + list(near_copies.values()) + sum(far_copies.values(), []):
        copy.wait_send()
    for copy in moved:
        copy.wait()

    mate = partner[walk]
    own_count = counts[walk]
    arriving = jnp.maximum(counts[mate] - LIVE, 0)
    distance = jnp.bitwise_xor(mate, walk)

    def arrived(offset, size):
        value = moved_in[0, pl.ds(offset, size)].astype(jnp.float32)
        for bit in range(1, bit_count):
            other = moved_in[bit, pl.ds(offset, size)].astype(jnp.float32)
            value = pick(distance == 1 << bit, other, value)
        return value

    came_rows = [arrived(move * (own_rows + TAIL), own_rows) for move in range(MOVE)]
    came_logs = [split_log(arrived(move * (own_rows + TAIL) + own_rows, TAIL)) for move in range(MOVE)]
    for slot in range(LIVE):
        result, weight = jnp.zeros((own_rows, occ), jnp.float32), jnp.zeros((LOG_ROWS, occ), jnp.float32)
        for move in range(MOVE):
            flag = (slot - own_count == move) & (move < arriving)
            result = pick(flag, came_rows[move], result)
            weight = pick(flag, came_logs[move], weight)
        flag = slot < jnp.minimum(own_count, LIVE)
        new_out[slot] = pick(flag, mine[slot], result).astype(jnp.bfloat16)
        weight = pick(flag, logs[slot], weight)
        log_out[slot] = weight[0, 0]


def shards(walkers, inv_intersection, fields, cholesky, trial_rows, counts, partner):
    chol_count = lax.axis_size("chol")
    bit_count = lax.axis_size("walk").bit_length() - 1
    slots, depth, occ = walkers.shape
    vectors, rows, orbitals = cholesky.shape
    own_rows = rows // chol_count
    half = chol_count // 2
    others = half - 1
    bf16, f32 = jnp.bfloat16, jnp.float32
    dma = pltpu.SemaphoreType.DMA
    anywhere = pl.BlockSpec(memory_space=pl.ANY)
    vmem = pl.BlockSpec(memory_space=pltpu.VMEM)
    smem = pl.BlockSpec(memory_space=pltpu.SMEM)
    return pl.pallas_call(
        functools.partial(kernel, chol_count, bit_count),
        out_shape=(
            jax.ShapeDtypeStruct((LIVE, own_rows, occ), bf16),
            jax.ShapeDtypeStruct((LIVE,), f32),
        ),
        in_specs=[anywhere, anywhere, vmem, anywhere, anywhere, smem, smem],
        out_specs=(vmem, smem),
        scratch_shapes=[
            pltpu.VMEM((slots, chol_count, depth, occ), bf16),
            pltpu.VMEM((vectors, rows, orbitals), bf16),
            pltpu.VMEM((slots, occ, occ), bf16),
            pltpu.VMEM((rows, occ), bf16),
            pltpu.VMEM((slots, vectors * rows, occ), f32),
            pltpu.VMEM((slots, rows, occ), f32),
            pltpu.VMEM((slots, chol_count, own_rows, occ), f32),
            pltpu.VMEM((slots, LOG_ROWS, occ), f32),
            pltpu.VMEM((slots, own_rows, occ), f32),
            pltpu.VMEM((slots, half * own_rows + LOG_ROWS, occ), f32),
            pltpu.VMEM((slots, half * own_rows + LOG_ROWS, occ), f32),
            pltpu.VMEM((slots, others, own_rows + TAIL, occ), bf16),
            pltpu.VMEM((slots, others, own_rows + TAIL, occ), bf16),
            pltpu.VMEM((MOVE * (own_rows + TAIL), occ), bf16),
            pltpu.VMEM((bit_count, MOVE * (own_rows + TAIL), occ), bf16),
            dma((4,)),
            dma((2,)),
            dma((slots, others)),
            dma((slots, others)),
            dma((slots, others)),
            dma((slots, others)),
            dma((slots,)),
            dma((slots,)),
            dma((slots, others)),
            dma((slots, others)),
            dma((bit_count,)),
            dma((bit_count,)),
        ],
        compiler_params=pltpu.CompilerParams(
            collective_id=0, has_side_effects=True, vmem_limit_bytes=48 << 20
        ),
        cost_estimate=pl.CostEstimate(
            flops=2 * slots * vectors * rows * orbitals * occ,
            bytes_accessed=2 * (walkers.size + cholesky.size),
            transcendentals=0,
        ),
    )(walkers, inv_intersection, fields, cholesky, trial_rows, counts, partner)


def solution(mesh):
    in_specs = (
        P("walk", "chol", None),
        P("walk", None, None),
        P("walk", "chol"),
        P("chol", None, None),
        P(),
        P(),
        P(),
    )
    out_specs = (P("walk", "chol", None), P("walk"))
    return jax.shard_map(shards, mesh=mesh, in_specs=in_specs, out_specs=out_specs, check_vma=False)
```

time: 91.9 us -> 43.9 us (0.48)
  waiting for transfers between devices: 37.5 us -> 0 us
  Pallas kernels: 0 us -> 35.2 us
  between operations: 18.1 us -> 0.64 us
  starting transfers between devices: 11 us -> 0 us
  matrix products: 6.23 us -> 0 us
  other arithmetic: 6.05 us -> 0 us
  blocking collectives: 5.9 us -> 0 us
    pallas_call x0 -> x1, Pallas kernels: none -> 35.2 us  [shards(): pl.pallas_call(functools.partial(kernel, chol_count, bit_count), out_shap...]
    all_gather x1 -> x0, waiting for transfers between devices: 31.1 us -> none  [propagate(): lax.all_gather(walker_rows, 'chol', axis=1, tiled=True)]
    ppermute x6 -> x0, starting transfers between devices: 10.9 us -> none  [from_partner(): return lax.ppermute(block, axis, route)]
    dot_general x3 -> x0, matrix products: 6.23 us -> none  [the longest x1 3.7 us: propagate(): jnp.einsum('grk,wkn->wgrn', cholesky, lax.all_gather(walker_rows, 'chol',...]
    psum x1 -> x0, blocking collectives: 5.9 us -> none  [propagate(): log_terms = lax.psum(weight_terms, 'chol')]
    unnamed x16 -> x15, local copies, waits for them, and re-layouts: 3.72 us -> 7.7 us
    reduce_scatter x1 -> x0, waiting for transfers between devices: 3.4 us -> none  [propagate(): lax.psum_scatter(row_terms, 'chol', scatter_dimension=1, tiled=True)]
    ppermute x6 -> x0, waiting for transfers between devices: 2.98 us -> none  [from_partner(): return lax.ppermute(block, axis, route)]
  transfers between devices with their start and end apart: 8 -> 0, of which waited for: 4 -> 0; matrix products, arithmetic and copies ran while one was open for 5% -> 0% of each run, Pallas kernels for 0% -> 0%
where the time goes in v1:
time: 43.9 us; the launch traced here: 43.6 us
  Pallas kernels  35.2 us (80%)
  local copies, waits for them, and re-layouts  7.7 us (18%)
  between operations  0.64 us (1%)
    pallas_call x1, Pallas kernels, shards(): pl.pallas_call(functools.partial(kernel, chol_count, bit_count), out_shap...  35.2 us
    unnamed x15, local copies, waits for them, and re-layouts  7.7 us

profile of v1, /device:TPU:0, one launch (start us, length us, event | category | flops | bytes accessed | tf_op | source)
XLA Modules:
  0.0 43.6 jit_solution(10103307200645281117)
XLA Ops:
  0.6 0.8 %copy.9.fields = bf16[6,2]{1,0:T(8,128)(2,1)S(1)} copy(bf16[6,2]{0,1:T(2,128)(2,1)} %param.9) | data formatting | bytes 48 | tf_op args[2]
  1.4 0.0 copy-start
  1.4 1.6 %copy-done = bf16[2,256,2048]{2,1,0:T(8,128)(2,1)S(1)} copy-done((bf16[2,256,2048]{2,1,0:T(8,128)(2,1)S(1)}, bf16[2,256,2048]{2,1,0:T(8,128)(2,1)}, u32[]{:S(2)}) %copy-start) | copy-done | bytes 2097176
  3.0 0.0 copy-start.1
  3.0 1.1 %copy-done.1 = bf16[6,512,128]{2,1,0:T(8,128)(2,1)S(1)} copy-done((bf16[6,512,128]{2,1,0:T(8,128)(2,1)S(1)}, bf16[6,512,128]{2,1,0:T(8,128)(2,1)}, u32[]{:S(2)}) %copy-start.1) | copy-done | bytes 786456
  4.1 0.0 copy-start.2
  4.1 0.9 %copy-done.2 = bf16[6,128,128]{2,1,0:T(8,128)(2,1)S(1)} copy-done((bf16[6,128,128]{2,1,0:T(8,128)(2,1)S(1)}, bf16[6,128,128]{2,1,0:T(8,128)(2,1)}, u32[]{:S(2)}) %copy-start.2) | copy-done | bytes 196632
  5.0 0.0 copy-start.3
  5.0 0.8 %copy-done.3 = bf16[256,128]{1,0:T(8,128)(2,1)S(1)} copy-done((bf16[256,128]{1,0:T(8,128)(2,1)S(1)}, bf16[256,128]{1,0:T(8,128)(2,1)}, u32[]{:S(2)}) %copy-start.3) | copy-done | bytes 65560
  5.9 0.0 copy-start.4
  5.9 0.7 %copy-done.4 = s32[8]{0:T(128)S(1)} copy-done((s32[8]{0:T(128)S(1)}, s32[8]{0:T(128)}, u32[]{:S(2)}) %copy-start.4) | copy-done | bytes 56
  6.5 0.0 copy-start.5
  6.5 0.7 %copy-done.5 = s32[8]{0:T(128)S(1)} copy-done((s32[8]{0:T(128)S(1)}, s32[8]{0:T(128)}, u32[]{:S(2)}) %copy-start.5) | copy-done | bytes 56
  7.2 35.2 %shard_map.86 = (bf16[4,64,128]{2,1,0:T(8,128)(2,1)S(1)}, f32[4]{0:T(128)S(1)}) custom-call(bf16[6,512,128]{2,1,0:T(8,128)(2,1)S(1)} %copy-done.1, bf16[6,128,128]{2,1,0:T(8,128)(2,1)S(1)} %copy-done.2, bf16[6,2]{1,0:T(8,128)(2,1)S(1)} %copy.9.fields, bf16[2,256,2048]{2,1,0:T(8,128)(2,1)S(1)} %copy-done, bf16[256,128]{1,0:T(8,128)(2,1)S(1)} %copy-done.3, ...), custom_call_target="tpu_custom_call" | custom-call | flops 1610612736 | bytes 2883584 | tf_op jit(solution)/shard_map/pallas_call | solution.py:290
  42.4 0.6 %copy.12 = bf16[4,64,128]{2,1,0:T(8,128)(2,1)} copy(bf16[4,64,128]{2,1,0:T(8,128)(2,1)S(1)} %get-tuple-element.4) | data formatting | bytes 131072
  43.1 0.5 %copy.13 = f32[4]{0:T(128)} copy(f32[4]{0:T(128)S(1)} %get-tuple-element.5) | data formatting | bytes 32
Async XLA Ops:
  1.4 1.6 %copy-start = (bf16[2,256,2048]{2,1,0:T(8,128)(2,1)S(1)}, bf16[2,256,2048]{2,1,0:T(8,128)(2,1)}, u32[]{:S(2)}) copy-start(bf16[2,256,2048]{2,1,0:T(8,128)(2,1)} %chol_in.1) | copy-start | bytes 6291460
  3.0 1.1 %copy-start.1 = (bf16[6,512,128]{2,1,0:T(8,128)(2,1)S(1)}, bf16[6,512,128]{2,1,0:T(8,128)(2,1)}, u32[]{:S(2)}) copy-start(bf16[6,512,128]{2,1,0:T(8,128)(2,1)} %walkers.1) | copy-start | bytes 2359300
  4.1 0.9 %copy-start.2 = (bf16[6,128,128]{2,1,0:T(8,128)(2,1)S(1)}, bf16[6,128,128]{2,1,0:T(8,128)(2,1)}, u32[]{:S(2)}) copy-start(bf16[6,128,128]{2,1,0:T(8,128)(2,1)} %minv_in.1) | copy-start | bytes 589828
  5.0 0.8 %copy-start.3 = (bf16[256,128]{1,0:T(8,128)(2,1)S(1)}, bf16[256,128]{1,0:T(8,128)(2,1)}, u32[]{:S(2)}) copy-start(bf16[256,128]{1,0:T(8,128)(2,1)} %trial_in.1) | copy-start | bytes 196612
  5.9 0.7 %copy-start.4 = (s32[8]{0:T(128)S(1)}, s32[8]{0:T(128)}, u32[]{:S(2)}) copy-start(s32[8]{0:T(128)} %counts.1) | copy-start | bytes 100
  6.5 0.7 %copy-start.5 = (s32[8]{0:T(128)S(1)}, s32[8]{0:T(128)}, u32[]{:S(2)}) copy-start(s32[8]{0:T(128)} %partner.1) | copy-start | bytes 100

commit v2 on v1

--- a/solution.py
+++ b/solution.py
@@ -9,6 +9,8 @@
 
 LIVE = 4
 MOVE = 2
+DEPTH = 3
+LAG = 4
 STEP_ROOT = 0.1
 LOG_ROWS = 8
 TAIL = 2 * LOG_ROWS
@@ -103,6 +105,8 @@
                 ahead_recv.at[slot, step],
                 {"chol": far_ids[step]},
             )
+    for slot in order[:DEPTH]:
+        for step in range(half - 1):
             ahead[slot, step].start()
     near = remote(walkers, phi.at[:, me], near_sem.at[0], near_sem.at[1], {"chol": sibling})
     near.start()
@@ -142,6 +146,9 @@
                 remote(block, block, pass_send.at[slot, step], pass_recv.at[slot, step], {"chol": sibling})
             )
             passed[step].start()
+            following = order.index(slot) + DEPTH
+            if following < slots:
+                ahead[order[following], step].start()
         total = prod[slot]
         for step in range(half - 1):
             passed[step].wait_recv()
@@ -155,7 +162,7 @@
         weight = jnp.zeros((1, 1), jnp.float32)
         for vector in range(vectors):
             force_bias = -STEP_ROOT * jnp.sum(total[vector] * weighted[slot], keepdims=True)
-            field = field_wide[slot : slot + 1, vector : vector + 1]
+            field = field_wide[vector : vector + 1, slot : slot + 1]
             increment += (STEP_ROOT * (field - force_bias)) * total[vector]
             weight += field * force_bias - 0.5 * force_bias * force_bias
         terms[slot] = increment.reshape(chol_count, own_rows, occ)
@@ -228,8 +235,8 @@
         if position - 1 >= 0 and position - 1 < slots:
             slot = order[position - 1]
             far_copies[slot] = add_chip(slot, near_copies[slot])
-        if position - 2 >= 0:
-            slot = order[position - 2]
+        if 0 <= position - LAG < slots:
+            slot = order[position - LAG]
             finish(slot, far_copies[slot])
             if slot == slots - 1:
                 for copy in moved:
@@ -240,8 +247,8 @@
         passed, near_copies[slot] = multiply(slot)
         sent += passed
         later(position)
-    later(slots)
-    later(slots + 1)
+    for position in range(slots, slots + LAG):
+        later(position)
 
     for copy in sent + list(near_copies.values()) + sum(far_copies.values(), []):
         copy.wait_send()
@@ -325,14 +332,14 @@
             dma((bit_count,)),
         ],
         compiler_params=pltpu.CompilerParams(
-            collective_id=0, has_side_effects=True, vmem_limit_bytes=48 << 20
+            collective_id=0, has_side_effects=True, vmem_limit_bytes=60 << 20
         ),
         cost_estimate=pl.CostEstimate(
             flops=2 * slots * vectors * rows * orbitals * occ,
             bytes_accessed=2 * (walkers.size + cholesky.size),
             transcendentals=0,
         ),
-    )(walkers, inv_intersection, fields, cholesky, trial_rows, counts, partner)
+    )(walkers, inv_intersection, fields.T, cholesky, trial_rows, counts, partner)
 
 
 def solution(mesh):

time: 43.9 us -> 35.4 us (0.81)
  local copies, waits for them, and re-layouts: 7.7 us -> 2.59 us
  Pallas kernels: 35.2 us -> 32 us
    unnamed x15 -> x2, local copies, waits for them, and re-layouts: 7.7 us -> 2.59 us
    pallas_call x1, Pallas kernels: 35.2 us -> 32 us  [shards(): pl.pallas_call(functools.partial(kernel, chol_count, bit_count), out_shap...]
where the time goes in v2:
time: 35.4 us; the launch traced here: 35.2 us
  Pallas kernels  32 us (90%)
  local copies, waits for them, and re-layouts  2.59 us (7%)
  between operations  0.64 us (2%)
    pallas_call x1, Pallas kernels, shards(): pl.pallas_call(functools.partial(kernel, chol_count, bit_count), out_shap...  32 us
    unnamed x2, local copies, waits for them, and re-layouts  2.59 us

profile of v2, /device:TPU:0, one launch (start us, length us, event | category | flops | bytes accessed | tf_op | source)
XLA Modules:
  0.0 35.2 jit_solution(15372098586665099100)
XLA Ops:
  0.6 32.0 %shard_map.86 = (bf16[4,64,128]{2,1,0:T(8,128)(2,1)}, f32[4]{0:T(128)}) custom-call(bf16[6,512,128]{2,1,0:T(8,128)(2,1)} %walkers.1, bf16[6,128,128]{2,1,0:T(8,128)(2,1)} %minv_in.1, bf16[2,6]{1,0:T(2,128)(2,1)} %bitcast.1, bf16[2,256,2048]{2,1,0:T(8,128)(2,1)} %chol_in.1, bf16[256,128]{1,0:T(8,128)(2,1)} %trial_in.1, s32[8]{0:T(128)} %counts.1, s32[8]{0:T(128)} %partner.1), custom_call_target="tpu_custom_call" | custom-call | flops 1610612736 | bytes 2883584 | tf_op jit(solution)/shard_map/pallas_call | solution.py:297
  32.6 1.5 %copy.11 = bf16[4,64,128]{2,1,0:T(8,128)(2,1)} copy(bf16[4,64,128]{2,1,0:T(8,128)(2,1)} %get-tuple-element.4) | data formatting | bytes 131072
  34.1 1.1 %copy.12 = f32[4]{0:T(128)} copy(f32[4]{0:T(128)} %get-tuple-element.5) | data formatting | bytes 32

commit v3 on v1

v3 whole, which is shorter than its diff:
```python
import functools

import jax
import jax.numpy as jnp
from jax import lax
from jax.experimental import pallas as pl
from jax.experimental.pallas import tpu as pltpu
from jax.sharding import PartitionSpec as P

LIVE = 4
MOVE = 2
PIECES = (1, 1, 1, 2)
VMEM_BYTES = 60 << 20
STEP_ROOT = 0.1
LOG_ROWS = 8
TAIL = 2 * LOG_ROWS
MESH = pl.DeviceIdType.MESH


def pick(flag, chosen, other):
    mask = jnp.broadcast_to(flag.astype(jnp.int32), chosen.shape) > 0
    return jnp.where(mask, chosen, other)


def kernel(
    chol_count,
    bit_count,
    walkers,
    minv_in,
    fields,
    chol_in,
    trial_in,
    counts,
    partner,
    new_out,
    log_out,
    phi,
    kept,
    came,
    chol,
    minv,
    came_minv,
    field_out,
    came_field,
    trial,
    prod,
    weighted,
    terms,
    logs,
    mine,
    sib_out,
    sib_in,
    far_out,
    far_in,
    load_sem,
    came_send,
    came_recv,
    minv_send,
    minv_recv,
    field_send,
    field_recv,
    near_send,
    near_recv,
    ahead_send,
    ahead_recv,
    pass_send,
    pass_recv,
    sib_send,
    sib_recv,
    far_send,
    far_recv,
):
    slots, depth, occ = walkers.shape
    vectors, rows, _ = chol_in.shape
    own_rows = rows // chol_count
    half = chol_count // 2
    walk = lax.axis_index("walk")
    me = lax.axis_index("chol")
    high, low = me // 2, me % 2
    sibling = 2 * high + 1 - low
    far_ids = [2 * lax.rem(high + step, half) + low for step in range(1, half)]
    from_high = [lax.rem(high - step + half, half) for step in range(1, half)]
    mates = [jnp.bitwise_xor(walk, 1 << bit) for bit in range(bit_count)]
    staying = LIVE - MOVE

    loads = [
        pltpu.make_async_copy(walkers.at[pl.ds(0, staying)], phi.at[pl.ds(0, staying), me], load_sem.at[0]),
        pltpu.make_async_copy(chol_in, chol, load_sem.at[1]),
        pltpu.make_async_copy(minv_in, minv, load_sem.at[2]),
        pltpu.make_async_copy(trial_in, trial, load_sem.at[3]),
        pltpu.make_async_copy(walkers.at[pl.ds(staying, MOVE)], kept, load_sem.at[4]),
    ]
    for load in loads:
        load.start()

    barrier = pltpu.get_barrier_semaphore()
    peers = [{"chol": sibling}] + [{"chol": far} for far in far_ids] + [{"walk": mate} for mate in mates]
    for peer in peers:
        pl.semaphore_signal(barrier, inc=1, device_id=peer, device_id_type=MESH)

    field_wide = fields[...].astype(jnp.float32)
    line = lax.broadcasted_iota(jnp.int32, field_out.shape, 0)
    spread = jnp.zeros(field_out.shape, jnp.float32)
    for move in range(MOVE):
        for vector in range(vectors):
            value = field_wide[vector : vector + 1, LIVE + move : LIVE + move + 1]
            spread = jnp.where(line == move * vectors + vector, value, spread)
    field_out[...] = spread.astype(jnp.bfloat16)

    pl.semaphore_wait(barrier, len(peers))

    def remote(src, dst, send, recv, peer):
        return pltpu.make_async_remote_copy(
            src_ref=src, dst_ref=dst, send_sem=send, recv_sem=recv, device_id=peer, device_id_type=MESH
        )

    def pieces(slot):
        count = PIECES[slot]
        return [(piece, pl.ds(piece * (depth // count), depth // count)) for piece in range(count)]

    sent = []

    def begin(copies):
        for copy in copies:
            copy.start()
        sent.extend(copies)
        return copies

    def send_ahead(slot, piece, span, source):
        return begin(
            [
                remote(
                    source,
                    phi.at[slot, me, span],
                    ahead_send.at[slot, step, piece],
                    ahead_recv.at[slot, step, piece],
                    {"chol": far_ids[step]},
                )
                for step in range(half - 1)
            ]
        )

    def send_near(slot, piece, span, source):
        return begin(
            [
                remote(
                    source,
                    phi.at[slot, me, span],
                    near_send.at[slot, piece],
                    near_recv.at[slot, piece],
                    {"chol": sibling},
                )
            ]
        )

    ahead, near, moved = {}, {}, {}

    def send_moved(move):
        for piece, span in pieces(staying + move):
            for bit in reversed(range(bit_count)):
                moved[move, piece, bit] = begin(
                    [
                        remote(
                            walkers.at[LIVE + move, span],
                            came.at[bit, move, span],
                            came_send.at[bit, move, piece],
                            came_recv.at[bit, move, piece],
                            {"walk": mates[bit]},
                        )
                    ]
                )[0]

    def send_own(slot):
        for piece, span in pieces(slot):
            ahead[slot, piece] = send_ahead(slot, piece, span, walkers.at[slot, span])
            near[slot, piece] = send_near(slot, piece, span, walkers.at[slot, span])

    send_own(0)
    send_moved(0)
    for slot in range(1, staying):
        send_own(slot)
    for move in range(1, MOVE):
        send_moved(move)
    small = []
    for bit in range(bit_count):
        small += begin(
            [
                remote(
                    minv_in.at[pl.ds(LIVE, MOVE)],
                    came_minv.at[bit],
                    minv_send.at[bit],
                    minv_recv.at[bit],
                    {"walk": mates[bit]},
                ),
                remote(
                    field_out, came_field.at[bit], field_send.at[bit], field_recv.at[bit], {"walk": mates[bit]}
                ),
            ]
        )

    mate = partner[walk]
    own_count = counts[walk]
    arriving = jnp.maximum(counts[mate] - LIVE, 0)
    distance = jnp.bitwise_xor(mate, walk)

    def arrived(read):
        value = read(0)
        for bit in range(1, bit_count):
            value = pick(distance == 1 << bit, read(bit), value)
        return value

    def place(move, read_came, read_own):
        value = read_own(move)
        for earlier in range(move):
            value = pick(own_count == LIVE - move + earlier, read_own(earlier), value)
        return pick(own_count < LIVE - move, arrived(lambda bit: read_came(bit, move)), value)

    def chol_half(index):
        columns = pl.ds(pl.multiple_of(index * 2 * depth, 2 * depth), 2 * depth)
        return chol[:, :, columns].reshape(vectors * rows, 2 * depth)

    def phi_half(slot, index):
        return phi[slot, pl.ds(2 * index, 2)].reshape(2 * depth, occ)

    def weigh(slot, inverse):
        weighted[slot] = lax.dot_general(
            trial[...], inverse, (((1,), (1,)), ((), ())), preferred_element_type=jnp.float32
        )

    def own_half(first):
        both = jnp.concatenate([phi_half(first, high), phi_half(first + 1, high)], axis=1)
        result = jnp.dot(chol_half(high), both, preferred_element_type=jnp.float32)
        prod[first] = result[:, :occ]
        prod[first + 1] = result[:, occ:]

    def forward(slot):
        passed = []
        for piece, span in pieces(slot):
            for step in range(half - 1):
                ahead[slot, piece][step].wait_recv()
                block = phi.at[slot, 2 * from_high[step] + low, span]
                passed += begin(
                    [
                        remote(
                            block,
                            block,
                            pass_send.at[slot, step, piece],
                            pass_recv.at[slot, step, piece],
                            {"chol": sibling},
                        )
                    ]
                )
        return passed

    def multiply(slot, passed, fields_of):
        for copy in passed:
            copy.wait_recv()
        total = prod[slot]
        for step in range(half - 1):
            total += jnp.dot(
                chol_half(from_high[step]),
                phi_half(slot, from_high[step]),
                preferred_element_type=jnp.float32,
            )
        total = total.reshape(vectors, rows, occ)
        increment = jnp.zeros((rows, occ), jnp.float32)
        weight = jnp.zeros((1, 1), jnp.float32)
        for vector in range(vectors):
            force_bias = -STEP_ROOT * jnp.sum(total[vector] * weighted[slot], keepdims=True)
            field = fields_of(vector)
            increment += (STEP_ROOT * (field - force_bias)) * total[vector]
            weight += field * force_bias - 0.5 * force_bias * force_bias
        terms[slot] = increment.reshape(chol_count, own_rows, occ)
        logs[slot] = jnp.broadcast_to(weight, (LOG_ROWS, occ))
        for index in range(half):
            sib_out[slot, pl.ds(index * own_rows, own_rows)] = terms[slot, 2 * index + 1 - low]
        sib_out[slot, pl.ds(half * own_rows, LOG_ROWS)] = logs[slot]
        return begin(
            [remote(sib_out.at[slot], sib_in.at[slot], sib_send.at[slot], sib_recv.at[slot], {"chol": sibling})]
        )[0]

    def chip_sum(slot, index):
        start = pl.multiple_of(index * own_rows, own_rows)
        return terms[slot, 2 * index + low] + sib_in[slot, pl.ds(start, own_rows)]

    def add_chip(slot, copy):
        copy.wait_recv()
        weight = logs[slot] + sib_in[slot, pl.ds(half * own_rows, LOG_ROWS)]
        logs[slot] = weight
        coarse = weight.astype(jnp.bfloat16).astype(jnp.float32)
        tail = jnp.concatenate([coarse, weight - coarse], axis=0).astype(jnp.bfloat16)
        copies = []
        for step in range(half - 1):
            far_out[slot, step, pl.ds(0, own_rows)] = chip_sum(slot, lax.rem(high + step + 1, half)).astype(
                jnp.bfloat16
            )
            far_out[slot, step, pl.ds(own_rows, TAIL)] = tail
            copies += begin(
                [
                    remote(
                        far_out.at[slot, step],
                        far_in.at[slot, step],
                        far_send.at[slot, step],
                        far_recv.at[slot, step],
                        {"chol": far_ids[step]},
                    )
                ]
            )
        mine[slot] = chip_sum(slot, high) + phi[slot, me, pl.ds(0, own_rows)].astype(jnp.float32)
        return copies

    def finish(slot, copies):
        result, weight = mine[slot], logs[slot]
        for step in range(half - 1):
            copies[step].wait_recv()
            result += far_in[slot, step, pl.ds(0, own_rows)].astype(jnp.float32)
            tail = far_in[slot, step, pl.ds(own_rows, TAIL)].astype(jnp.float32)
            weight += tail[:LOG_ROWS] + tail[LOG_ROWS:]
        return result, weight

    def place_walker(move):
        slot = staying + move
        for piece, span in pieces(slot):
            for bit in range(bit_count):
                moved[move, piece, bit].wait_recv()
            phi[slot, me, span] = place(
                move, lambda bit, move: came[bit, move, span], lambda own: kept[own, span]
            )
            source = phi.at[slot, me, span]
            ahead[slot, piece] = send_ahead(slot, piece, span, source)
            near[slot, piece] = send_near(slot, piece, span, source)

    def wait_near(slot):
        for piece, _ in pieces(slot):
            near[slot, piece][0].wait_recv()

    def own_field(slot):
        return lambda vector: field_wide[vector : vector + 1, slot : slot + 1]

    def placed_field(move):
        def of(vector):
            def read_came(bit, move):
                index = move * vectors + vector
                return came_field[bit].astype(jnp.float32)[index : index + 1, :1]

            return place(move, read_came, lambda own: own_field(staying + own)(vector))

        return of

    for load in loads[2:4]:
        load.wait()
    for slot in range(staying):
        weigh(slot, minv[slot])
    for load in loads[:2]:
        load.wait()
    for slot in range(staying):
        wait_near(slot)
    own_half(0)
    near_sum, far_sum = {}, {}
    passed = {0: forward(0)}
    near_sum[0] = multiply(0, passed[0], own_field(0))
    loads[4].wait()
    place_walker(0)
    passed[1] = forward(1)
    near_sum[1] = multiply(1, passed[1], own_field(1))
    far_sum[0] = add_chip(0, near_sum[0])
    place_walker(1)
    far_sum[1] = add_chip(1, near_sum[1])
    for copy in small:
        copy.wait_recv()
    for move in range(MOVE):
        weigh(
            staying + move,
            place(move, lambda bit, move: came_minv[bit, move], lambda own: minv[staying + own]),
        )
    wait_near(2)
    wait_near(3)
    own_half(2)
    passed[2] = forward(2)
    near_sum[2] = multiply(2, passed[2], placed_field(0))
    passed[3] = forward(3)
    far_sum[2] = add_chip(2, near_sum[2])
    near_sum[3] = multiply(3, passed[3], placed_field(1))
    done = [finish(slot, far_sum[slot]) for slot in range(2)]
    far_sum[3] = add_chip(3, near_sum[3])
    done += [finish(slot, far_sum[slot]) for slot in range(2, LIVE)]

    def balanced(index):
        first, second, third, fourth = [done[slot][index] for slot in range(LIVE)]
        return [
            first,
            pick(own_count == 1, third, second),
            pick((own_count == 2) | (own_count >= LIVE), third, fourth),
            pick(own_count == 3, third, fourth),
        ]

    new_rows, new_logs = balanced(0), balanced(1)
    for slot in range(LIVE):
        came_here = slot - own_count
        live = (slot < jnp.minimum(own_count, LIVE)) | ((came_here >= 0) & (came_here < arriving))
        new_out[slot] = pick(live, new_rows[slot], jnp.zeros_like(new_rows[slot])).astype(jnp.bfloat16)
        log_out[slot] = pick(live, new_logs[slot], jnp.zeros_like(new_logs[slot]))[0, 0]

    for copy in sent:
        copy.wait_send()


def shards(walkers, inv_intersection, fields, cholesky, trial_rows, counts, partner):
    chol_count = lax.axis_size("chol")
    bit_count = lax.axis_size("walk").bit_length() - 1
    slots, depth, occ = walkers.shape
    vectors, rows, orbitals = cholesky.shape
    own_rows = rows // chol_count
    half = chol_count // 2
    others = half - 1
    most = max(PIECES)
    field_rows = -(-MOVE * vectors // 16) * 16
    bf16, f32 = jnp.bfloat16, jnp.float32
    dma = pltpu.SemaphoreType.DMA
    anywhere = pl.BlockSpec(memory_space=pl.ANY)
    vmem = pl.BlockSpec(memory_space=pltpu.VMEM)
    smem = pl.BlockSpec(memory_space=pltpu.SMEM)
    return pl.pallas_call(
        functools.partial(kernel, chol_count, bit_count),
        out_shape=(
            jax.ShapeDtypeStruct((LIVE, own_rows, occ), bf16),
            jax.ShapeDtypeStruct((LIVE,), f32),
        ),
        in_specs=[anywhere, anywhere, vmem, anywhere, anywhere, smem, smem],
        out_specs=(vmem, smem),
        scratch_shapes=[
            pltpu.VMEM((LIVE, chol_count, depth, occ), bf16),
            pltpu.VMEM((MOVE, depth, occ), bf16),
            pltpu.VMEM((bit_count, MOVE, depth, occ), bf16),
            pltpu.VMEM((vectors, rows, orbitals), bf16),
            pltpu.VMEM((slots, occ, occ), bf16),
            pltpu.VMEM((bit_count, MOVE, occ, occ), bf16),
            pltpu.VMEM((field_rows, occ), bf16),
            pltpu.VMEM((bit_count, field_rows, occ), bf16),
            pltpu.VMEM((rows, occ), bf16),
            pltpu.VMEM((LIVE, vectors * rows, occ), f32),
            pltpu.VMEM((LIVE, rows, occ), f32),
            pltpu.VMEM((LIVE, chol_count, own_rows, occ), f32),
            pltpu.VMEM((LIVE, LOG_ROWS, occ), f32),
            pltpu.VMEM((LIVE, own_rows, occ), f32),
            pltpu.VMEM((LIVE, half * own_rows + LOG_ROWS, occ), f32),
            pltpu.VMEM((LIVE, half * own_rows + LOG_ROWS, occ), f32),
            pltpu.VMEM((LIVE, others, own_rows + TAIL, occ), bf16),
            pltpu.VMEM((LIVE, others, own_rows + TAIL, occ), bf16),
            dma((5,)),
            dma((bit_count, MOVE, most)),
            dma((bit_count, MOVE, most)),
            dma((bit_count,)),
            dma((bit_count,)),
            dma((bit_count,)),
            dma((bit_count,)),
            dma((LIVE, most)),
            dma((LIVE, most)),
            dma((LIVE, others, most)),
            dma((LIVE, others, most)),
            dma((LIVE, others, most)),
            dma((LIVE, others, most)),
            dma((LIVE,)),
            dma((LIVE,)),
            dma((LIVE, others)),
            dma((LIVE, others)),
        ],
        compiler_params=pltpu.CompilerParams(
            collective_id=0, has_side_effects=True, vmem_limit_bytes=VMEM_BYTES
        ),
        cost_estimate=pl.CostEstimate(
            flops=2 * LIVE * vectors * rows * orbitals * occ,
            bytes_accessed=2 * (walkers.size + cholesky.size),
            transcendentals=0,
        ),
    )(walkers, inv_intersection, fields.T, cholesky, trial_rows, counts, partner)


def solution(mesh):
    in_specs = (
        P("walk", "chol", None),
        P("walk", None, None),
        P("walk", "chol"),
        P("chol", None, None),
        P(),
        P(),
        P(),
    )
    out_specs = (P("walk", "chol", None), P("walk"))
    return jax.shard_map(shards, mesh=mesh, in_specs=in_specs, out_specs=out_specs, check_vma=False)
```

time: 43.9 us -> 35.4 us (0.81)
  local copies, waits for them, and re-layouts: 7.7 us -> 2.59 us
  Pallas kernels: 35.2 us -> 32 us
    unnamed x15 -> x2, local copies, waits for them, and re-layouts: 7.7 us -> 2.59 us
    pallas_call x1, Pallas kernels: 35.2 us -> 32 us  [shards(): pl.pallas_call(functools.partial(kernel, chol_count, bit_count), out_shap...]
where the time goes in v3:
time: 35.4 us; the launch traced here: 35.2 us
  Pallas kernels  32 us (90%)
  local copies, waits for them, and re-layouts  2.59 us (7%)
  between operations  0.64 us (2%)
    pallas_call x1, Pallas kernels, shards(): pl.pallas_call(functools.partial(kernel, chol_count, bit_count), out_shap...  32 us
    unnamed x2, local copies, waits for them, and re-layouts  2.59 us

profile of v3, /device:TPU:0, one launch (start us, length us, event | category | flops | bytes accessed | tf_op | source)
XLA Modules:
  0.0 35.2 jit_solution(15605022030093934216)
XLA Ops:
  0.6 32.0 %shard_map.86 = (bf16[4,64,128]{2,1,0:T(8,128)(2,1)}, f32[4]{0:T(128)}) custom-call(bf16[6,512,128]{2,1,0:T(8,128)(2,1)} %walkers.1, bf16[6,128,128]{2,1,0:T(8,128)(2,1)} %minv_in.1, bf16[2,6]{1,0:T(2,128)(2,1)} %bitcast.1, bf16[2,256,2048]{2,1,0:T(8,128)(2,1)} %chol_in.1, bf16[256,128]{1,0:T(8,128)(2,1)} %trial_in.1, s32[8]{0:T(128)} %counts.1, s32[8]{0:T(128)} %partner.1), custom_call_target="tpu_custom_call" | custom-call | flops 1073741824 | bytes 2883584 | tf_op jit(solution)/shard_map/pallas_call | solution.py:423
  32.6 1.5 %copy.11 = bf16[4,64,128]{2,1,0:T(8,128)(2,1)} copy(bf16[4,64,128]{2,1,0:T(8,128)(2,1)} %get-tuple-element.4) | data formatting | bytes 131072
  34.1 1.1 %copy.12 = f32[4]{0:T(128)} copy(f32[4]{0:T(128)} %get-tuple-element.5) | data formatting | bytes 32

commit v4 on v1

v4 whole, which is shorter than its diff:
```python
import functools

import jax
import jax.numpy as jnp
from jax import lax
from jax.experimental import pallas as pl
from jax.experimental.pallas import tpu as pltpu
from jax.sharding import PartitionSpec as P

LIVE = 4
MOVE = 2
DEPTH = 2
VMEM_BYTES = 40 << 20
STEP_ROOT = 0.1
LOG_ROWS = 8
TAIL = 2 * LOG_ROWS
MESH = pl.DeviceIdType.MESH


def pick(flag, chosen, other):
    mask = jnp.broadcast_to(flag.astype(jnp.int32), chosen.shape) > 0
    return jnp.where(mask, chosen, other)


def kernel(
    chol_count,
    bit_count,
    walkers,
    minv_in,
    fields,
    chol_in,
    trial_in,
    counts,
    partner,
    new_out,
    log_out,
    phi,
    window,
    chol,
    minv,
    field_all,
    trial,
    prod,
    terms,
    base,
    sib_out,
    far_out,
    far_in,
    done,
    done_logs,
    moved_out,
    moved_in,
    load_sem,
    swap_send,
    swap_recv,
    near_send,
    near_recv,
    ahead_send,
    ahead_recv,
    sib_send,
    sib_recv,
    far_send,
    far_recv,
    moved_send,
    moved_recv,
):
    slots, depth, occ = walkers.shape
    vectors, rows, _ = chol_in.shape
    own_rows = rows // chol_count
    half = chol_count // 2
    pairs = slots // 2
    walk = lax.axis_index("walk")
    me = lax.axis_index("chol")
    high, low = me // 2, me % 2
    sibling = 2 * high + 1 - low
    to_high = [lax.rem(high + step, half) for step in range(1, half)]
    from_high = [lax.rem(high - step + half, half) for step in range(1, half)]
    mates = [jnp.bitwise_xor(walk, 1 << bit) for bit in range(bit_count)]
    fars = [(step, core) for step in range(half - 1) for core in range(2)]

    loads = [
        pltpu.make_async_copy(chol_in, chol.at[pl.ds(low * vectors, vectors)], load_sem.at[0]),
        pltpu.make_async_copy(minv_in, minv, load_sem.at[1]),
        pltpu.make_async_copy(trial_in, trial, load_sem.at[2]),
        pltpu.make_async_copy(walkers.at[:, pl.ds(0, own_rows)], window, load_sem.at[3]),
    ]
    own_loads = [
        pltpu.make_async_copy(walkers.at[2 * pair + low], phi.at[pair, me], load_sem.at[4 + pair])
        for pair in range(pairs)
    ]
    for load in loads + own_loads:
        load.start()

    barrier = pltpu.get_barrier_semaphore()
    peers = [{"chol": sibling}] + [{"chol": 2 * to_high[step] + core} for step, core in fars]
    peers += [{"walk": mate} for mate in mates]
    for peer in peers:
        pl.semaphore_signal(barrier, inc=1, device_id=peer, device_id_type=MESH)

    field_wide = fields[...].astype(jnp.float32)
    line = lax.broadcasted_iota(jnp.int32, field_all.shape[1:], 0)
    spread = jnp.zeros(field_all.shape[1:], jnp.float32)
    for slot in range(slots):
        for vector in range(vectors):
            value = field_wide[vector : vector + 1, slot : slot + 1]
            spread = jnp.where(line == slot * vectors + vector, value, spread)
    field_all[low] = spread.astype(jnp.bfloat16)

    pl.semaphore_wait(barrier, len(peers))

    def remote(src, dst, send, recv, peer):
        return pltpu.make_async_remote_copy(
            src_ref=src, dst_ref=dst, send_sem=send, recv_sem=recv, device_id=peer, device_id_type=MESH
        )

    sent = []

    def begin(copy):
        copy.start()
        sent.append(copy)
        return copy

    def send_ahead(pair):
        for step, core in fars:
            begin(
                remote(
                    walkers.at[2 * pair + core],
                    phi.at[pair, me],
                    ahead_send.at[pair, step, core],
                    ahead_recv.at[pair, step, low],
                    {"chol": 2 * to_high[step] + core},
                )
            )

    def wait_ahead(pair):
        for step, core in fars:
            remote(
                walkers.at[0],
                phi.at[pair, 2 * from_high[step] + core],
                ahead_send.at[pair, step, core],
                ahead_recv.at[pair, step, core],
                {"chol": sibling},
            ).wait_recv()

    order = list(range(LIVE // 2, pairs)) + list(range(LIVE // 2))
    for pair in order[:DEPTH]:
        send_ahead(pair)
    own_chol = pl.ds(low * vectors, vectors)
    swaps = [
        begin(remote(field_all.at[low], field_all.at[low], swap_send.at[0], swap_recv.at[0], {"chol": sibling})),
        begin(remote(chol_in, chol.at[own_chol], swap_send.at[1], swap_recv.at[1], {"chol": sibling})),
    ]
    near = [
        begin(
            remote(
                walkers.at[2 * pair + 1 - low],
                phi.at[pair, me],
                near_send.at[pair],
                near_recv.at[pair],
                {"chol": sibling},
            )
        )
        for pair in range(pairs)
    ]

    def chol_half(index):
        columns = pl.ds(pl.multiple_of(index * 2 * depth, 2 * depth), 2 * depth)
        return chol[:, :, columns].reshape(2 * vectors * rows, 2 * depth)

    def phi_half(pair, index):
        return phi[pair, pl.ds(2 * index, 2)].reshape(2 * depth, occ)

    for load in loads + own_loads:
        load.wait()
    for copy in near + swaps:
        copy.wait_recv()
    every = jnp.concatenate([phi_half(pair, high) for pair in range(pairs)], axis=1)
    result = jnp.dot(chol_half(high), every, preferred_element_type=jnp.float32)
    for pair in range(pairs):
        prod[pair] = result[:, pair * occ : (pair + 1) * occ]

    def multiply(pair):
        weighted = lax.dot_general(
            trial[...], minv[2 * pair + low], (((1,), (1,)), ((), ())), preferred_element_type=jnp.float32
        )
        wait_ahead(pair)
        later = order.index(pair) + DEPTH
        if later < pairs:
            send_ahead(order[later])
        total = prod[pair]
        for step in range(half - 1):
            total += jnp.dot(
                chol_half(from_high[step]),
                phi_half(pair, from_high[step]),
                preferred_element_type=jnp.float32,
            )
        total = total.reshape(2 * vectors, rows, occ)
        increment = jnp.zeros((rows, occ), jnp.float32)
        weight = jnp.zeros((1, 1), jnp.float32)
        for vector in range(2 * vectors):
            force_bias = -STEP_ROOT * jnp.sum(total[vector] * weighted, keepdims=True)
            values = field_all[vector // vectors].astype(jnp.float32)
            first = 2 * pair * vectors + vector % vectors
            field = pick(
                low == 0, values[first : first + 1, :1], values[first + vectors : first + vectors + 1, :1]
            )
            increment += (STEP_ROOT * (field - force_bias)) * total[vector]
            weight += field * force_bias - 0.5 * force_bias * force_bias
        terms[pair] = increment.reshape(chol_count, own_rows, occ)
        weight = jnp.broadcast_to(weight, (LOG_ROWS, occ))
        tail = split(weight)
        for step, core in fars:
            target = 2 * to_high[step] + core
            far_out[pair, step, core, pl.ds(0, own_rows)] = terms[pair, target].astype(jnp.bfloat16)
            far_out[pair, step, core, pl.ds(own_rows, TAIL)] = tail
            begin(
                remote(
                    far_out.at[pair, step, core],
                    far_in.at[pair, step, low],
                    far_send.at[pair, step, core],
                    far_recv.at[pair, step, low],
                    {"chol": target},
                )
            )
        sib_out[pair, pl.ds(0, own_rows)] = terms[pair, sibling]
        sib_out[pair, pl.ds(own_rows, LOG_ROWS)] = weight
        base[pair, low, pl.ds(0, own_rows)] = terms[pair, me]
        base[pair, low, pl.ds(own_rows, LOG_ROWS)] = weight
        begin(
            remote(
                sib_out.at[pair], base.at[pair, low], sib_send.at[pair], sib_recv.at[pair], {"chol": sibling}
            )
        )

    def split(weight):
        coarse = weight.astype(jnp.bfloat16).astype(jnp.float32)
        return jnp.concatenate([coarse, weight - coarse], axis=0).astype(jnp.bfloat16)

    def joined(tail):
        return tail[:LOG_ROWS] + tail[LOG_ROWS:]

    moved = [
        remote(moved_out, moved_in.at[bit], moved_send.at[bit], moved_recv.at[bit], {"walk": mates[bit]})
        for bit in range(bit_count)
    ]

    def finish(pair):
        remote(
            sib_out.at[pair], base.at[pair, 1 - low], sib_send.at[pair], sib_recv.at[pair], {"chol": sibling}
        ).wait_recv()
        for step, core in fars:
            remote(
                far_out.at[pair, step, core],
                far_in.at[pair, step, core],
                far_send.at[pair, step, core],
                far_recv.at[pair, step, core],
                {"chol": sibling},
            ).wait_recv()
        for core in range(2):
            slot = 2 * pair + core
            result = window[slot].astype(jnp.float32) + base[pair, core, pl.ds(0, own_rows)]
            weight = base[pair, core, pl.ds(own_rows, LOG_ROWS)]
            for step in range(half - 1):
                result += far_in[pair, step, core, pl.ds(0, own_rows)].astype(jnp.float32)
                weight += joined(far_in[pair, step, core, pl.ds(own_rows, TAIL)].astype(jnp.float32))
            if slot < LIVE:
                done[slot] = result
                done_logs[slot] = weight
            else:
                start = (slot - LIVE) * (own_rows + TAIL)
                moved_out[pl.ds(start, own_rows)] = result.astype(jnp.bfloat16)
                moved_out[pl.ds(start + own_rows, TAIL)] = split(weight)
        if pair == pairs - 1:
            for copy in moved:
                begin(copy)

    for position, pair in enumerate(order):
        multiply(pair)
        if position == 1:
            finish(order[0])
    for pair in order[1:]:
        finish(pair)

    mate = partner[walk]
    own_count = counts[walk]
    arriving = jnp.maximum(counts[mate] - LIVE, 0)
    distance = jnp.bitwise_xor(mate, walk)
    for copy in moved:
        copy.wait_recv()

    def arrived(offset, size):
        value = moved_in[0, pl.ds(offset, size)].astype(jnp.float32)
        for bit in range(1, bit_count):
            other = moved_in[bit, pl.ds(offset, size)].astype(jnp.float32)
            value = pick(distance == 1 << bit, other, value)
        return value

    came_rows = [arrived(move * (own_rows + TAIL), own_rows) for move in range(MOVE)]
    came_logs = [joined(arrived(move * (own_rows + TAIL) + own_rows, TAIL)) for move in range(MOVE)]
    for slot in range(LIVE):
        result, weight = jnp.zeros((own_rows, occ), jnp.float32), jnp.zeros((LOG_ROWS, occ), jnp.float32)
        for move in range(MOVE):
            flag = (slot - own_count == move) & (move < arriving)
            result = pick(flag, came_rows[move], result)
            weight = pick(flag, came_logs[move], weight)
        flag = slot < jnp.minimum(own_count, LIVE)
        new_out[slot] = pick(flag, done[slot], result).astype(jnp.bfloat16)
        weight = pick(flag, done_logs[slot], weight)
        log_out[slot] = weight[0, 0]

    for copy in sent:
        copy.wait_send()


def shards(walkers, inv_intersection, fields, cholesky, trial_rows, counts, partner):
    chol_count = lax.axis_size("chol")
    bit_count = lax.axis_size("walk").bit_length() - 1
    slots, depth, occ = walkers.shape
    vectors, rows, orbitals = cholesky.shape
    own_rows = rows // chol_count
    others = chol_count // 2 - 1
    pairs = slots // 2
    field_rows = -(-slots * vectors // 16) * 16
    bf16, f32 = jnp.bfloat16, jnp.float32
    dma = pltpu.SemaphoreType.DMA
    anywhere = pl.BlockSpec(memory_space=pl.ANY)
    vmem = pl.BlockSpec(memory_space=pltpu.VMEM)
    smem = pl.BlockSpec(memory_space=pltpu.SMEM)
    operands = (walkers, inv_intersection, fields.T, cholesky, trial_rows, counts, partner)
    operands = [pltpu.with_memory_space_constraint(operand, pltpu.HBM) for operand in operands]
    return pl.pallas_call(
        functools.partial(kernel, chol_count, bit_count),
        out_shape=(
            jax.ShapeDtypeStruct((LIVE, own_rows, occ), bf16),
            jax.ShapeDtypeStruct((LIVE,), f32),
        ),
        in_specs=[anywhere, anywhere, vmem, anywhere, anywhere, smem, smem],
        out_specs=(vmem, smem),
        scratch_shapes=[
            pltpu.VMEM((pairs, chol_count, depth, occ), bf16),
            pltpu.VMEM((slots, own_rows, occ), bf16),
            pltpu.VMEM((2 * vectors, rows, orbitals), bf16),
            pltpu.VMEM((slots, occ, occ), bf16),
            pltpu.VMEM((2, field_rows, occ), bf16),
            pltpu.VMEM((rows, occ), bf16),
            pltpu.VMEM((pairs, 2 * vectors * rows, occ), f32),
            pltpu.VMEM((pairs, chol_count, own_rows, occ), f32),
            pltpu.VMEM((pairs, 2, own_rows + LOG_ROWS, occ), f32),
            pltpu.VMEM((pairs, own_rows + LOG_ROWS, occ), f32),
            pltpu.VMEM((pairs, others, 2, own_rows + TAIL, occ), bf16),
            pltpu.VMEM((pairs, others, 2, own_rows + TAIL, occ), bf16),
            pltpu.VMEM((LIVE, own_rows, occ), f32),
            pltpu.VMEM((LIVE, LOG_ROWS, occ), f32),
            pltpu.VMEM((MOVE * (own_rows + TAIL), occ), bf16),
            pltpu.VMEM((bit_count, MOVE * (own_rows + TAIL), occ), bf16),
            dma((4 + pairs,)),
            dma((2,)),
            dma((2,)),
            dma((pairs,)),
            dma((pairs,)),
            dma((pairs, others, 2)),
            dma((pairs, others, 2)),
            dma((pairs,)),
            dma((pairs,)),
            dma((pairs, others, 2)),
            dma((pairs, others, 2)),
            dma((bit_count,)),
            dma((bit_count,)),
        ],
        compiler_params=pltpu.CompilerParams(
            collective_id=0, has_side_effects=True, vmem_limit_bytes=VMEM_BYTES
        ),
        cost_estimate=pl.CostEstimate(
            flops=2 * slots * vectors * rows * orbitals * occ,
            bytes_accessed=2 * (walkers.size + cholesky.size),
            transcendentals=0,
        ),
    )(*operands)


def solution(mesh):
    in_specs = (
        P("walk", "chol", None),
        P("walk", None, None),
        P("walk", "chol"),
        P("chol", None, None),
        P(),
        P(),
        P(),
    )
    out_specs = (P("walk", "chol", None), P("walk"))
    return jax.shard_map(shards, mesh=mesh, in_specs=in_specs, out_specs=out_specs, check_vma=False)
```

time: 43.9 us -> 32.5 us (0.74)
  local copies, waits for them, and re-layouts: 7.7 us -> 1.14 us
  Pallas kernels: 35.2 us -> 30.5 us
    unnamed x15 -> x2, local copies, waits for them, and re-layouts: 7.7 us -> 1.14 us
    pallas_call x1, Pallas kernels: 35.2 us -> 30.5 us  [shards(): pl.pallas_call(functools.partial(kernel, chol_count, bit_count), out_shap...]
where the time goes in v4:
time: 32.5 us; the launch traced here: 32.3 us
  Pallas kernels  30.5 us (94%)
  local copies, waits for them, and re-layouts  1.14 us (4%)
  between operations  0.64 us (2%)
    pallas_call x1, Pallas kernels, shards(): pl.pallas_call(functools.partial(kernel, chol_count, bit_count), out_shap...  30.5 us
    unnamed x2, local copies, waits for them, and re-layouts  1.14 us

profile of v4, /device:TPU:0, one launch (start us, length us, event | category | flops | bytes accessed | tf_op | source)
XLA Modules:
  0.0 32.3 jit_solution(4313810807143642041)
XLA Ops:
  0.6 30.5 %shard_map.86 = (bf16[4,64,128]{2,1,0:T(8,128)(2,1)S(1)}, f32[4]{0:T(128)S(1)}) custom-call(bf16[6,512,128]{2,1,0:T(8,128)(2,1)} %walkers.1, bf16[6,128,128]{2,1,0:T(8,128)(2,1)} %minv_in.1, bf16[2,6]{1,0:T(2,128)(2,1)} %bitcast.1, bf16[2,256,2048]{2,1,0:T(8,128)(2,1)} %chol_in.1, bf16[256,128]{1,0:T(8,128)(2,1)} %trial_in.1, s32[8]{0:T(128)} %counts.1, ...), custom_call_target="tpu_custom_call" | custom-call | flops 1610612736 | bytes 2883584 | tf_op jit(solution)/shard_map/pallas_call | solution.py:331
  31.1 0.6 %copy.11 = bf16[4,64,128]{2,1,0:T(8,128)(2,1)} copy(bf16[4,64,128]{2,1,0:T(8,128)(2,1)S(1)} %get-tuple-element.4) | data formatting | bytes 131072
  31.8 0.5 %copy.12 = f32[4]{0:T(128)} copy(f32[4]{0:T(128)S(1)} %get-tuple-element.5) | data formatting | bytes 32

commit v5 on v4

--- a/solution.py
+++ b/solution.py
@@ -8,8 +8,6 @@
 from jax.sharding import PartitionSpec as P
 
 LIVE = 4
-MOVE = 2
-DEPTH = 2
 VMEM_BYTES = 40 << 20
 STEP_ROOT = 0.1
 LOG_ROWS = 8
@@ -36,9 +34,14 @@
     log_out,
     phi,
     window,
+    kept,
+    placed,
+    came,
     chol,
     minv,
+    came_minv,
     field_all,
+    came_field,
     trial,
     prod,
     terms,
@@ -51,6 +54,8 @@
     moved_out,
     moved_in,
     load_sem,
+    came_send,
+    came_recv,
     swap_send,
     swap_recv,
     near_send,
@@ -83,6 +88,7 @@
         pltpu.make_async_copy(minv_in, minv, load_sem.at[1]),
         pltpu.make_async_copy(trial_in, trial, load_sem.at[2]),
         pltpu.make_async_copy(walkers.at[:, pl.ds(0, own_rows)], window, load_sem.at[3]),
+        pltpu.make_async_copy(walkers.at[LIVE - 1], kept, load_sem.at[4 + pairs]),
     ]
     own_loads = [
         pltpu.make_async_copy(walkers.at[2 * pair + low], phi.at[pair, me], load_sem.at[4 + pair])
@@ -120,15 +126,15 @@
         sent.append(copy)
         return copy
 
-    def send_ahead(pair):
-        for step, core in fars:
+    def send_ahead(slot, source):
+        for step in range(half - 1):
             begin(
                 remote(
-                    walkers.at[2 * pair + core],
-                    phi.at[pair, me],
-                    ahead_send.at[pair, step, core],
-                    ahead_recv.at[pair, step, low],
-                    {"chol": 2 * to_high[step] + core},
+                    source,
+                    phi.at[slot // 2, me],
+                    ahead_send.at[slot // 2, step, slot % 2],
+                    ahead_recv.at[slot // 2, step, low],
+                    {"chol": 2 * to_high[step] + slot % 2},
                 )
             )
 
@@ -142,26 +148,86 @@
                 {"chol": sibling},
             ).wait_recv()
 
-    order = list(range(LIVE // 2, pairs)) + list(range(LIVE // 2))
-    for pair in order[:DEPTH]:
-        send_ahead(pair)
-    own_chol = pl.ds(low * vectors, vectors)
+    def near_copy(pair, source):
+        return remote(source, phi.at[pair, me], near_send.at[pair], near_recv.at[pair], {"chol": sibling})
+
+    home, last = LIVE // 2, LIVE // 2 - 1
+    send_ahead(LIVE, walkers.at[LIVE])
+    moves = [
+        begin(
+            remote(
+                walkers.at[LIVE + 1],
+                came.at[bit],
+                came_send.at[0, bit],
+                came_recv.at[0, bit],
+                {"walk": mates[bit]},
+            )
+        )
+        for bit in reversed(range(bit_count))
+    ]
+    send_ahead(0, walkers.at[0])
+    send_ahead(1, walkers.at[1])
     swaps = [
         begin(remote(field_all.at[low], field_all.at[low], swap_send.at[0], swap_recv.at[0], {"chol": sibling})),
-        begin(remote(chol_in, chol.at[own_chol], swap_send.at[1], swap_recv.at[1], {"chol": sibling})),
-    ]
-    near = [
         begin(
             remote(
-                walkers.at[2 * pair + 1 - low],
-                phi.at[pair, me],
-                near_send.at[pair],
-                near_recv.at[pair],
+                chol_in,
+                chol.at[pl.ds(low * vectors, vectors)],
+                swap_send.at[1],
+                swap_recv.at[1],
                 {"chol": sibling},
             )
-        )
-        for pair in range(pairs)
-    ]
+        ),
+    ]
+    near = [near_copy(pair, walkers.at[2 * pair + 1 - low]) for pair in range(last)]
+    for copy in near:
+        begin(copy)
+
+    @pl.when(low == 1)
+    def _():
+        near_copy(home, walkers.at[LIVE]).start()
+        near_copy(last, walkers.at[LIVE - 2]).start()
+
+    moves += [
+        begin(
+            remote(
+                minv_in.at[LIVE + 1],
+                came_minv.at[bit],
+                came_send.at[1, bit],
+                came_recv.at[1, bit],
+                {"walk": mates[bit]},
+            )
+        )
+        for bit in range(bit_count)
+    ]
+    swaps[0].wait_recv()
+    moves += [
+        begin(
+            remote(
+                field_all,
+                came_field.at[bit],
+                came_send.at[2, bit],
+                came_recv.at[2, bit],
+                {"walk": mates[bit]},
+            )
+        )
+        for bit in range(bit_count)
+    ]
+    send_ahead(LIVE - 2, walkers.at[LIVE - 2])
+
+    mate = partner[walk]
+    own_count = counts[walk]
+    arriving = jnp.maximum(counts[mate] - LIVE, 0)
+    distance = jnp.bitwise_xor(mate, walk)
+
+    def arrived(read):
+        value = read(0)
+        for bit in range(1, bit_count):
+            value = pick(distance == 1 << bit, read(bit), value)
+        return value
+
+    def place(own, read):
+        return pick(own_count < LIVE, arrived(read), own)
 
     def chol_half(index):
         columns = pl.ds(pl.multiple_of(index * 2 * depth, 2 * depth), 2 * depth)
@@ -172,21 +238,70 @@
 
     for load in loads + own_loads:
         load.wait()
-    for copy in near + swaps:
+    for copy in near + swaps[1:]:
         copy.wait_recv()
-    every = jnp.concatenate([phi_half(pair, high) for pair in range(pairs)], axis=1)
-    result = jnp.dot(chol_half(high), every, preferred_element_type=jnp.float32)
-    for pair in range(pairs):
-        prod[pair] = result[:, pair * occ : (pair + 1) * occ]
+
+    @pl.when(low == 0)
+    def _():
+        near_copy(home, walkers.at[LIVE]).wait_recv()
+
+    def own_half(some):
+        every = jnp.concatenate([phi_half(pair, high) for pair in some], axis=1)
+        result = jnp.dot(chol_half(high), every, preferred_element_type=jnp.float32)
+        for index, pair in enumerate(some):
+            prod[pair] = result[:, index * occ : (index + 1) * occ]
+
+    own_half([home] + list(range(last)))
+
+    def place_last():
+        for copy in moves:
+            copy.wait_recv()
+        placed[...] = place(kept[...], lambda bit: came[bit])
+        send_ahead(LIVE - 1, placed)
+
+        @pl.when(low == 0)
+        def _():
+            near_copy(last, placed).start()
+
+        phi[last, me] = pick(low == 1, placed[...], phi[last, me])
+
+    def field_of(pair, vector):
+        values = field_all[vector // vectors].astype(jnp.float32)
+        place_in = vector % vectors
+
+        def at(array, slot):
+            line = slot * vectors + place_in
+            return array[line : line + 1, :1]
+
+        second = at(values, 2 * pair + 1)
+        if pair == last:
+            second = place(
+                second, lambda bit: at(came_field[bit, vector // vectors].astype(jnp.float32), LIVE + 1)
+            )
+        return pick(low == 0, at(values, 2 * pair), second)
+
+    def far_copy(pair, step, core):
+        return remote(
+            far_out.at[pair, step, core],
+            far_in.at[pair, step, low],
+            far_send.at[pair, step, core],
+            far_recv.at[pair, step, low],
+            {"chol": 2 * to_high[step] + core},
+        )
+
+    def sib_copy(pair):
+        return remote(
+            sib_out.at[pair], base.at[pair, low], sib_send.at[pair], sib_recv.at[pair], {"chol": sibling}
+        )
 
     def multiply(pair):
+        inverse = minv[2 * pair + low]
+        if pair == last:
+            inverse = pick(low == 0, inverse, place(minv[LIVE - 1], lambda bit: came_minv[bit]))
         weighted = lax.dot_general(
-            trial[...], minv[2 * pair + low], (((1,), (1,)), ((), ())), preferred_element_type=jnp.float32
+            trial[...], inverse, (((1,), (1,)), ((), ())), preferred_element_type=jnp.float32
         )
         wait_ahead(pair)
-        later = order.index(pair) + DEPTH
-        if later < pairs:
-            send_ahead(order[later])
         total = prod[pair]
         for step in range(half - 1):
             total += jnp.dot(
@@ -199,11 +314,7 @@
         weight = jnp.zeros((1, 1), jnp.float32)
         for vector in range(2 * vectors):
             force_bias = -STEP_ROOT * jnp.sum(total[vector] * weighted, keepdims=True)
-            values = field_all[vector // vectors].astype(jnp.float32)
-            first = 2 * pair * vectors + vector % vectors
-            field = pick(
-                low == 0, values[first : first + 1, :1], values[first + vectors : first + vectors + 1, :1]
-            )
+            field = field_of(pair, vector)
             increment += (STEP_ROOT * (field - force_bias)) * total[vector]
             weight += field * force_bias - 0.5 * force_bias * force_bias
         terms[pair] = increment.reshape(chol_count, own_rows, occ)
@@ -213,24 +324,12 @@
             target = 2 * to_high[step] + core
             far_out[pair, step, core, pl.ds(0, own_rows)] = terms[pair, target].astype(jnp.bfloat16)
             far_out[pair, step, core, pl.ds(own_rows, TAIL)] = tail
-            begin(
-                remote(
-                    far_out.at[pair, step, core],
-                    far_in.at[pair, step, low],
-                    far_send.at[pair, step, core],
-                    far_recv.at[pair, step, low],
-                    {"chol": target},
-                )
-            )
+            far_copy(pair, step, core).start()
         sib_out[pair, pl.ds(0, own_rows)] = terms[pair, sibling]
         sib_out[pair, pl.ds(own_rows, LOG_ROWS)] = weight
         base[pair, low, pl.ds(0, own_rows)] = terms[pair, me]
         base[pair, low, pl.ds(own_rows, LOG_ROWS)] = weight
-        begin(
-            remote(
-                sib_out.at[pair], base.at[pair, low], sib_send.at[pair], sib_recv.at[pair], {"chol": sibling}
-            )
-        )
+        sib_copy(pair).start()
 
     def split(weight):
         coarse = weight.astype(jnp.bfloat16).astype(jnp.float32)
@@ -245,20 +344,34 @@
     ]
 
     def finish(pair):
-        remote(
-            sib_out.at[pair], base.at[pair, 1 - low], sib_send.at[pair], sib_recv.at[pair], {"chol": sibling}
-        ).wait_recv()
-        for step, core in fars:
+        cores = 1 if pair == home else 2
+
+        def wait_sibling():
             remote(
-                far_out.at[pair, step, core],
-                far_in.at[pair, step, core],
-                far_send.at[pair, step, core],
-                far_recv.at[pair, step, core],
+                sib_out.at[pair],
+                base.at[pair, 1 - low],
+                sib_send.at[pair],
+                sib_recv.at[pair],
                 {"chol": sibling},
             ).wait_recv()
-        for core in range(2):
+
+        if pair == home:
+            pl.when(low == 1)(wait_sibling)
+        else:
+            wait_sibling()
+        for step, core in fars:
+            if core < cores:
+                remote(
+                    far_out.at[pair, step, core],
+                    far_in.at[pair, step, core],
+                    far_send.at[pair, step, core],
+                    far_recv.at[pair, step, core],
+                    {"chol": sibling},
+                ).wait_recv()
+        for core in range(cores):
             slot = 2 * pair + core
-            result = window[slot].astype(jnp.float32) + base[pair, core, pl.ds(0, own_rows)]
+            rows_in = placed[pl.ds(0, own_rows)] if slot == LIVE - 1 else window[slot]
+            result = rows_in.astype(jnp.float32) + base[pair, core, pl.ds(0, own_rows)]
             weight = base[pair, core, pl.ds(own_rows, LOG_ROWS)]
             for step in range(half - 1):
                 result += far_in[pair, step, core, pl.ds(0, own_rows)].astype(jnp.float32)
@@ -267,49 +380,55 @@
                 done[slot] = result
                 done_logs[slot] = weight
             else:
-                start = (slot - LIVE) * (own_rows + TAIL)
-                moved_out[pl.ds(start, own_rows)] = result.astype(jnp.bfloat16)
-                moved_out[pl.ds(start + own_rows, TAIL)] = split(weight)
-        if pair == pairs - 1:
+                moved_out[pl.ds(0, own_rows)] = result.astype(jnp.bfloat16)
+                moved_out[pl.ds(own_rows, TAIL)] = split(weight)
+        if pair == home:
             for copy in moved:
                 begin(copy)
 
-    for position, pair in enumerate(order):
+    pl.when(low == 0)(functools.partial(multiply, home))
+    place_last()
+    for pair in range(last):
         multiply(pair)
-        if position == 1:
-            finish(order[0])
-    for pair in order[1:]:
+    finish(home)
+    near_copy(last, placed).wait_recv()
+    own_half([last])
+    multiply(last)
+    for pair in range(home):
         finish(pair)
-
-    mate = partner[walk]
-    own_count = counts[walk]
-    arriving = jnp.maximum(counts[mate] - LIVE, 0)
-    distance = jnp.bitwise_xor(mate, walk)
     for copy in moved:
         copy.wait_recv()
 
-    def arrived(offset, size):
-        value = moved_in[0, pl.ds(offset, size)].astype(jnp.float32)
-        for bit in range(1, bit_count):
-            other = moved_in[bit, pl.ds(offset, size)].astype(jnp.float32)
-            value = pick(distance == 1 << bit, other, value)
-        return value
-
-    came_rows = [arrived(move * (own_rows + TAIL), own_rows) for move in range(MOVE)]
-    came_logs = [joined(arrived(move * (own_rows + TAIL) + own_rows, TAIL)) for move in range(MOVE)]
+    came_rows = arrived(lambda bit: moved_in[bit, pl.ds(0, own_rows)].astype(jnp.float32))
+    came_logs = joined(arrived(lambda bit: moved_in[bit, pl.ds(own_rows, TAIL)].astype(jnp.float32)))
+
+    def choose(slot, own, first, second):
+        came_here = slot - own_count
+        value = pick((came_here == 1) & (arriving > 1), second, jnp.zeros_like(own))
+        value = pick((came_here == 0) & (arriving > 0), first, value)
+        return pick(slot < jnp.minimum(own_count, LIVE), own, value)
+
     for slot in range(LIVE):
-        result, weight = jnp.zeros((own_rows, occ), jnp.float32), jnp.zeros((LOG_ROWS, occ), jnp.float32)
-        for move in range(MOVE):
-            flag = (slot - own_count == move) & (move < arriving)
-            result = pick(flag, came_rows[move], result)
-            weight = pick(flag, came_logs[move], weight)
-        flag = slot < jnp.minimum(own_count, LIVE)
-        new_out[slot] = pick(flag, done[slot], result).astype(jnp.bfloat16)
-        weight = pick(flag, done_logs[slot], weight)
-        log_out[slot] = weight[0, 0]
+        new_out[slot] = choose(slot, done[slot], came_rows, done[LIVE - 1]).astype(jnp.bfloat16)
+        log_out[slot] = choose(slot, done_logs[slot], came_logs, done_logs[LIVE - 1])[0, 0]
 
     for copy in sent:
         copy.wait_send()
+    near_copy(last, placed).wait_send()
+    for pair in range(home):
+        sib_copy(pair).wait_send()
+        for step, core in fars:
+            far_copy(pair, step, core).wait_send()
+
+    @pl.when(low == 0)
+    def _():
+        sib_copy(home).wait_send()
+        for step, core in fars:
+            far_copy(home, step, core).wait_send()
+
+    @pl.when(low == 1)
+    def _():
+        near_copy(home, walkers.at[LIVE]).wait_send()
 
 
 def shards(walkers, inv_intersection, fields, cholesky, trial_rows, counts, partner):
@@ -339,9 +458,14 @@
         scratch_shapes=[
             pltpu.VMEM((pairs, chol_count, depth, occ), bf16),
             pltpu.VMEM((slots, own_rows, occ), bf16),
+            pltpu.VMEM((depth, occ), bf16),
+            pltpu.VMEM((depth, occ), bf16),
+            pltpu.VMEM((bit_count, depth, occ), bf16),
             pltpu.VMEM((2 * vectors, rows, orbitals), bf16),
             pltpu.VMEM((slots, occ, occ), bf16),
+            pltpu.VMEM((bit_count, occ, occ), bf16),
             pltpu.VMEM((2, field_rows, occ), bf16),
+            pltpu.VMEM((bit_count, 2, field_rows, occ), bf16),
             pltpu.VMEM((rows, occ), bf16),
             pltpu.VMEM((pairs, 2 * vectors * rows, occ), f32),
             pltpu.VMEM((pairs, chol_count, own_rows, occ), f32),
@@ -351,9 +475,11 @@
             pltpu.VMEM((pairs, others, 2, own_rows + TAIL, occ), bf16),
             pltpu.VMEM((LIVE, own_rows, occ), f32),
             pltpu.VMEM((LIVE, LOG_ROWS, occ), f32),
-            pltpu.VMEM((MOVE * (own_rows + TAIL), occ), bf16),
-            pltpu.VMEM((bit_count, MOVE * (own_rows + TAIL), occ), bf16),
-            dma((4 + pairs,)),
+            pltpu.VMEM((own_rows + TAIL, occ), bf16),
+            pltpu.VMEM((bit_count, own_rows + TAIL, occ), bf16),
+            dma((5 + pairs,)),
+            dma((3, bit_count)),
+            dma((3, bit_count)),
             dma((2,)),
             dma((2,)),
             dma((pairs,)),

time: 32.5 us -> 28.1 us (0.86)
  Pallas kernels: 30.5 us -> 26.2 us
    pallas_call x1, Pallas kernels: 30.5 us -> 26.2 us  [shards(): pl.pallas_call(functools.partial(kernel, chol_count, bit_count), out_shap...]
where the time goes in v5:
time: 28.1 us; the launch traced here: 28 us
  Pallas kernels  26.2 us (93%)
  local copies, waits for them, and re-layouts  1.14 us (4%)
  between operations  0.64 us (2%)
    pallas_call x1, Pallas kernels, shards(): pl.pallas_call(functools.partial(kernel, chol_count, bit_count), out_shap...  26.2 us
    unnamed x2, local copies, waits for them, and re-layouts  1.14 us

profile of v5, /device:TPU:0, one launch (start us, length us, event | category | flops | bytes accessed | tf_op | source)
XLA Modules:
  0.0 28.0 jit_solution(9356470527172786649)
XLA Ops:
  0.6 26.2 %shard_map.86 = (bf16[4,64,128]{2,1,0:T(8,128)(2,1)S(1)}, f32[4]{0:T(128)S(1)}) custom-call(bf16[6,512,128]{2,1,0:T(8,128)(2,1)} %walkers.1, bf16[6,128,128]{2,1,0:T(8,128)(2,1)} %minv_in.1, bf16[2,6]{1,0:T(2,128)(2,1)} %bitcast.1, bf16[2,256,2048]{2,1,0:T(8,128)(2,1)} %chol_in.1, bf16[256,128]{1,0:T(8,128)(2,1)} %trial_in.1, s32[8]{0:T(128)} %counts.1, ...), custom_call_target="tpu_custom_call" | custom-call | flops 1610612736 | bytes 2883584 | tf_op jit(solution)/shard_map/pallas_call | solution.py:450
  26.8 0.6 %copy.11 = bf16[4,64,128]{2,1,0:T(8,128)(2,1)} copy(bf16[4,64,128]{2,1,0:T(8,128)(2,1)S(1)} %get-tuple-element.4) | data formatting | bytes 131072
  27.4 0.5 %copy.12 = f32[4]{0:T(128)} copy(f32[4]{0:T(128)S(1)} %get-tuple-element.5) | data formatting | bytes 32

commit v6 on v5

--- a/solution.py
+++ b/solution.py
@@ -28,10 +28,12 @@
     fields,
     chol_in,
     trial_in,
+    counts_in,
+    partner_in,
+    new_out,
+    log_out,
     counts,
     partner,
-    new_out,
-    log_out,
     phi,
     window,
     kept,
@@ -90,11 +92,15 @@
         pltpu.make_async_copy(walkers.at[:, pl.ds(0, own_rows)], window, load_sem.at[3]),
         pltpu.make_async_copy(walkers.at[LIVE - 1], kept, load_sem.at[4 + pairs]),
     ]
+    table_loads = [
+        pltpu.make_async_copy(counts_in, counts, load_sem.at[5 + pairs]),
+        pltpu.make_async_copy(partner_in, partner, load_sem.at[6 + pairs]),
+    ]
     own_loads = [
         pltpu.make_async_copy(walkers.at[2 * pair + low], phi.at[pair, me], load_sem.at[4 + pair])
         for pair in range(pairs)
     ]
-    for load in loads + own_loads:
+    for load in loads + own_loads + table_loads:
         load.start()
 
     barrier = pltpu.get_barrier_semaphore()
@@ -215,6 +221,8 @@
     ]
     send_ahead(LIVE - 2, walkers.at[LIVE - 2])
 
+    for load in table_loads:
+        load.wait()
     mate = partner[walk]
     own_count = counts[walk]
     arriving = jnp.maximum(counts[mate] - LIVE, 0)
@@ -301,6 +309,7 @@
         weighted = lax.dot_general(
             trial[...], inverse, (((1,), (1,)), ((), ())), preferred_element_type=jnp.float32
         )
+        field_values = [field_of(pair, vector) for vector in range(2 * vectors)]
         wait_ahead(pair)
         total = prod[pair]
         for step in range(half - 1):
@@ -314,7 +323,7 @@
         weight = jnp.zeros((1, 1), jnp.float32)
         for vector in range(2 * vectors):
             force_bias = -STEP_ROOT * jnp.sum(total[vector] * weighted, keepdims=True)
-            field = field_of(pair, vector)
+            field = field_values[vector]
             increment += (STEP_ROOT * (field - force_bias)) * total[vector]
             weight += field * force_bias - 0.5 * force_bias * force_bias
         terms[pair] = increment.reshape(chol_count, own_rows, occ)
@@ -390,9 +399,9 @@
     place_last()
     for pair in range(last):
         multiply(pair)
-    finish(home)
     near_copy(last, placed).wait_recv()
     own_half([last])
+    finish(home)
     multiply(last)
     for pair in range(home):
         finish(pair)
@@ -408,9 +417,13 @@
         value = pick((came_here == 0) & (arriving > 0), first, value)
         return pick(slot < jnp.minimum(own_count, LIVE), own, value)
 
+    lane = lax.broadcasted_iota(jnp.int32, (LOG_ROWS, occ), 1)
+    weights = jnp.zeros((LOG_ROWS, occ), jnp.float32)
     for slot in range(LIVE):
         new_out[slot] = choose(slot, done[slot], came_rows, done[LIVE - 1]).astype(jnp.bfloat16)
-        log_out[slot] = choose(slot, done_logs[slot], came_logs, done_logs[LIVE - 1])[0, 0]
+        weight = choose(slot, done_logs[slot], came_logs, done_logs[LIVE - 1])
+        weights = jnp.where(lane == slot, weight, weights)
+    log_out[...] = weights[0, :LIVE]
 
     for copy in sent:
         copy.wait_send()
@@ -444,7 +457,6 @@
     dma = pltpu.SemaphoreType.DMA
     anywhere = pl.BlockSpec(memory_space=pl.ANY)
     vmem = pl.BlockSpec(memory_space=pltpu.VMEM)
-    smem = pl.BlockSpec(memory_space=pltpu.SMEM)
     operands = (walkers, inv_intersection, fields.T, cholesky, trial_rows, counts, partner)
     operands = [pltpu.with_memory_space_constraint(operand, pltpu.HBM) for operand in operands]
     return pl.pallas_call(
@@ -453,9 +465,11 @@
             jax.ShapeDtypeStruct((LIVE, own_rows, occ), bf16),
             jax.ShapeDtypeStruct((LIVE,), f32),
         ),
-        in_specs=[anywhere, anywhere, vmem, anywhere, anywhere, smem, smem],
-        out_specs=(vmem, smem),
+        in_specs=[anywhere, anywhere, vmem, anywhere, anywhere, anywhere, anywhere],
+        out_specs=(vmem, vmem),
         scratch_shapes=[
+            pltpu.SMEM(counts.shape, jnp.int32),
+            pltpu.SMEM(partner.shape, jnp.int32),
             pltpu.VMEM((pairs, chol_count, depth, occ), bf16),
             pltpu.VMEM((slots, own_rows, occ), bf16),
             pltpu.VMEM((depth, occ), bf16),
@@ -477,7 +491,7 @@
             pltpu.VMEM((LIVE, LOG_ROWS, occ), f32),
             pltpu.VMEM((own_rows + TAIL, occ), bf16),
             pltpu.VMEM((bit_count, own_rows + TAIL, occ), bf16),
-            dma((5 + pairs,)),
+            dma((7 + pairs,)),
             dma((3, bit_count)),
             dma((3, bit_count)),
             dma((2,)),

time: 28.1 us -> 27.3 us (0.972)
  Pallas kernels: 26.2 us -> 25.4 us
    pallas_call x1, Pallas kernels: 26.2 us -> 25.4 us  [shards(): pl.pallas_call(functools.partial(kernel, chol_count, bit_count), out_shap...]
where the time goes in v6:
time: 27.3 us; the launch traced here: 27.1 us
  Pallas kernels  25.4 us (93%)
  local copies, waits for them, and re-layouts  1.14 us (4%)
  between operations  0.64 us (2%)
    pallas_call x1, Pallas kernels, shards(): pl.pallas_call(functools.partial(kernel, chol_count, bit_count), out_shap...  25.4 us
    unnamed x2, local copies, waits for them, and re-layouts  1.14 us

profile of v6, /device:TPU:0, one launch (start us, length us, event | category | flops | bytes accessed | tf_op | source)
XLA Modules:
  0.0 27.1 jit_solution(2684902186630563380)
XLA Ops:
  0.6 25.4 %shard_map.86 = (bf16[4,64,128]{2,1,0:T(8,128)(2,1)S(1)}, f32[4]{0:T(128)S(1)}) custom-call(bf16[6,512,128]{2,1,0:T(8,128)(2,1)} %walkers.1, bf16[6,128,128]{2,1,0:T(8,128)(2,1)} %minv_in.1, bf16[2,6]{1,0:T(2,128)(2,1)} %bitcast.1, bf16[2,256,2048]{2,1,0:T(8,128)(2,1)} %chol_in.1, bf16[256,128]{1,0:T(8,128)(2,1)} %trial_in.1, s32[8]{0:T(128)} %counts_in.1, ...), custom_call_target="tpu_custom_call" | custom-call | flops 1610612736 | bytes 2883584 | tf_op jit(solution)/shard_map/pallas_call | solution.py:462
  26.0 0.6 %copy.11 = bf16[4,64,128]{2,1,0:T(8,128)(2,1)} copy(bf16[4,64,128]{2,1,0:T(8,128)(2,1)S(1)} %get-tuple-element.4) | data formatting | bytes 131072
  26.6 0.5 %copy.12 = f32[4]{0:T(128)} copy(f32[4]{0:T(128)S(1)} %get-tuple-element.5) | data formatting | bytes 32

commit v7 on v6

--- a/solution.py
+++ b/solution.py
@@ -175,16 +175,20 @@
     send_ahead(1, walkers.at[1])
     swaps = [
         begin(remote(field_all.at[low], field_all.at[low], swap_send.at[0], swap_recv.at[0], {"chol": sibling})),
-        begin(
-            remote(
-                chol_in,
-                chol.at[pl.ds(low * vectors, vectors)],
-                swap_send.at[1],
-                swap_recv.at[1],
-                {"chol": sibling},
-            )
-        ),
-    ]
+    ]
+
+    def swap(step):
+        start = lax.rem(high + step, half) * 2 * depth
+        columns = pl.ds(pl.multiple_of(start, 2 * depth), 2 * depth)
+        return remote(
+            chol_in.at[:, :, columns],
+            chol.at[pl.ds(low * vectors, vectors), :, columns],
+            swap_send.at[1 + step],
+            swap_recv.at[1 + step],
+            {"chol": sibling},
+        )
+
+    swaps += [begin(swap(0))]
     near = [near_copy(pair, walkers.at[2 * pair + 1 - low]) for pair in range(last)]
     for copy in near:
         begin(copy)
@@ -194,6 +198,7 @@
         near_copy(home, walkers.at[LIVE]).start()
         near_copy(last, walkers.at[LIVE - 2]).start()
 
+    swaps += [begin(swap(step)) for step in range(1, half)]
     moves += [
         begin(
             remote(
@@ -219,7 +224,6 @@
         )
         for bit in range(bit_count)
     ]
-    send_ahead(LIVE - 2, walkers.at[LIVE - 2])
 
     for load in table_loads:
         load.wait()
@@ -246,7 +250,7 @@
 
     for load in loads + own_loads:
         load.wait()
-    for copy in near + swaps[1:]:
+    for copy in near + swaps[1:2]:
         copy.wait_recv()
 
     @pl.when(low == 0)
@@ -260,8 +264,11 @@
             prod[pair] = result[:, index * occ : (index + 1) * occ]
 
     own_half([home] + list(range(last)))
+    for copy in swaps[2:]:
+        copy.wait_recv()
 
     def place_last():
+        send_ahead(LIVE - 2, walkers.at[LIVE - 2])
         for copy in moves:
             copy.wait_recv()
         placed[...] = place(kept[...], lambda bit: came[bit])
@@ -494,8 +501,8 @@
             dma((7 + pairs,)),
             dma((3, bit_count)),
             dma((3, bit_count)),
-            dma((2,)),
-            dma((2,)),
+            dma((1 + chol_count // 2,)),
+            dma((1 + chol_count // 2,)),
             dma((pairs,)),
             dma((pairs,)),
             dma((pairs, others, 2)),

time: 27.3 us -> 27.3 us (level)
  no operation moved by 1% of the time
where the time goes in v7:
time: 27.3 us; the launch traced here: 27.2 us
  Pallas kernels  25.4 us (93%)
  local copies, waits for them, and re-layouts  1.14 us (4%)
  between operations  0.64 us (2%)
    pallas_call x1, Pallas kernels, shards(): pl.pallas_call(functools.partial(kernel, chol_count, bit_count), out_shap...  25.4 us
    unnamed x2, local copies, waits for them, and re-layouts  1.14 us

profile of v7, /device:TPU:0, one launch (start us, length us, event | category | flops | bytes accessed | tf_op | source)
XLA Modules:
  0.0 27.2 jit_solution(6987005269171807199)
XLA Ops:
  0.6 25.4 %shard_map.86 = (bf16[4,64,128]{2,1,0:T(8,128)(2,1)S(1)}, f32[4]{0:T(128)S(1)}) custom-call(bf16[6,512,128]{2,1,0:T(8,128)(2,1)} %walkers.1, bf16[6,128,128]{2,1,0:T(8,128)(2,1)} %minv_in.1, bf16[2,6]{1,0:T(2,128)(2,1)} %bitcast.1, bf16[2,256,2048]{2,1,0:T(8,128)(2,1)} %chol_in.1, bf16[256,128]{1,0:T(8,128)(2,1)} %trial_in.1, s32[8]{0:T(128)} %counts_in.1, ...), custom_call_target="tpu_custom_call" | custom-call | flops 1610612736 | bytes 2883584 | tf_op jit(solution)/shard_map/pallas_call | solution.py:469
  26.0 0.6 %copy.11 = bf16[4,64,128]{2,1,0:T(8,128)(2,1)} copy(bf16[4,64,128]{2,1,0:T(8,128)(2,1)S(1)} %get-tuple-element.4) | data formatting | bytes 131072
  26.7 0.5 %copy.12 = f32[4]{0:T(128)} copy(f32[4]{0:T(128)S(1)} %get-tuple-element.5) | data formatting | bytes 32

commit v8 on v7

--- a/solution.py
+++ b/solution.py
@@ -269,7 +269,7 @@
 
     def place_last():
         send_ahead(LIVE - 2, walkers.at[LIVE - 2])
-        for copy in moves:
+        for copy in moves[:bit_count]:
             copy.wait_recv()
         placed[...] = place(kept[...], lambda bit: came[bit])
         send_ahead(LIVE - 1, placed)
@@ -409,6 +409,8 @@
     near_copy(last, placed).wait_recv()
     own_half([last])
     finish(home)
+    for copy in moves[bit_count:]:
+        copy.wait_recv()
     multiply(last)
     for pair in range(home):
         finish(pair)

time: 27.3 us -> 27.3 us (level)
  no operation moved by 1% of the time
where the time goes in v8:
time: 27.3 us; the launch traced here: 27.2 us
  Pallas kernels  25.4 us (93%)
  local copies, waits for them, and re-layouts  1.14 us (4%)
  between operations  0.64 us (2%)
    pallas_call x1, Pallas kernels, shards(): pl.pallas_call(functools.partial(kernel, chol_count, bit_count), out_shap...  25.4 us
    unnamed x2, local copies, waits for them, and re-layouts  1.14 us

profile of v8, /device:TPU:0, one launch (start us, length us, event | category | flops | bytes accessed | tf_op | source)
XLA Modules:
  0.0 27.2 jit_solution(941911771064507789)
XLA Ops:
  0.6 25.4 %shard_map.86 = (bf16[4,64,128]{2,1,0:T(8,128)(2,1)S(1)}, f32[4]{0:T(128)S(1)}) custom-call(bf16[6,512,128]{2,1,0:T(8,128)(2,1)} %walkers.1, bf16[6,128,128]{2,1,0:T(8,128)(2,1)} %minv_in.1, bf16[2,6]{1,0:T(2,128)(2,1)} %bitcast.1, bf16[2,256,2048]{2,1,0:T(8,128)(2,1)} %chol_in.1, bf16[256,128]{1,0:T(8,128)(2,1)} %trial_in.1, s32[8]{0:T(128)} %counts_in.1, ...), custom_call_target="tpu_custom_call" | custom-call | flops 1610612736 | bytes 2883584 | tf_op jit(solution)/shard_map/pallas_call | solution.py:471
  26.0 0.6 %copy.11 = bf16[4,64,128]{2,1,0:T(8,128)(2,1)} copy(bf16[4,64,128]{2,1,0:T(8,128)(2,1)S(1)} %get-tuple-element.4) | data formatting | bytes 131072
  26.6 0.5 %copy.12 = f32[4]{0:T(128)} copy(f32[4]{0:T(128)S(1)} %get-tuple-element.5) | data formatting | bytes 32
